TPU v7x, 32 devices: a whole 2x2x4 slice. The times are simulated.
32 devices in a mesh: wide: 8 (over y, x, core), narrow: 4 (over z).
Axes of the slice: x: 2, y: 2, z: 4, core: 2. Of those that a mesh axis runs over, the one named last changes fastest.
Arguments:
- params: float32 [8, 4, 1024, 512], P('wide', 'narrow'), may hold values from -6 to 6
- public: float32 [8, 4, 1024, 512], P('wide', 'narrow'), may hold values from -6 to 6
- mixed: float32 [8, 4, 1024, 512], P('wide', 'narrow'), may hold values from -6 to 6
- inputs: bfloat16 [8, 4, 256, 1024], P('wide', 'narrow'), may hold values from -6 to 6
- cotangent: bfloat16 [8, 4, 256, 512], P('wide', 'narrow'), may hold values from -1.5 to 1.5
- block_ids: int32 [8, 4, 2, 8], P('wide', 'narrow'), may hold values from 0 to 31, as said below
- block_counts: int32 [8, 4, 2], P('wide', 'narrow'), may hold values from 1 to 8, as said below
Outputs:
- params_out: float32 [8, 4, 1024, 512], P('wide', 'narrow')
- public_out: float32 [8, 4, 1024, 512], P('wide', 'narrow')
- mixed_out: float32 [8, 4, 1024, 512], P('wide', 'narrow')
Inputs may be any that keep to these rules, and one draw needn't show every extreme that they name: `block_ids`: each row of 8 entries holds distinct tile numbers; entries past the row's count are unused. `block_counts`: some replica uses all 8 entries in some round in every draw.
All inputs are finite; a program needn't handle non-finite values.
Results may differ from a plain program's by a relative error of at most 0.0003.
Values sent between devices are 32-bit elements; how exact they have to be, the bound alone decides.
A program may use at most 128 MiB of HBM per device.

v0:
```python
import jax
import jax.numpy as jnp
from jax import lax
from jax.sharding import PartitionSpec as P

D = 1024
COLS = 512
TILE = 128


LEARN_RATE = 0.05
NEIGHBOUR_WEIGHT = 0.2
CONSENSUS = 0.4


def shifted(value, axis, steps):
    count = lax.axis_size(axis)
    pairs = [(source, (source + steps) % count) for source in range(count)]
    return lax.ppermute(value, axis, pairs)


def to_blocks(matrix):
    row_tiles = D // TILE
    col_tiles = COLS // TILE
    shaped = matrix.reshape(row_tiles, TILE, col_tiles, TILE)
    shaped = jnp.swapaxes(shaped, 1, 2)
    return shaped.reshape(row_tiles * col_tiles, TILE, TILE)


def from_blocks(blocks):
    row_tiles = D // TILE
    col_tiles = COLS // TILE
    shaped = blocks.reshape(row_tiles, col_tiles, TILE, TILE)
    shaped = jnp.swapaxes(shaped, 1, 2)
    return shaped.reshape(1, 1, D, COLS)


def on_device(params, public, mixed, inputs, cotangent, block_ids, block_counts):
    gradient = lax.dot_general(
        inputs[0, 0], cotangent[0, 0], (((0,), (0,)), ((), ())), preferred_element_type=jnp.float32
    )
    current = to_blocks(params[0, 0] - LEARN_RATE * gradient)
    public_blocks = to_blocks(public[0, 0])
    mixed_blocks = to_blocks(mixed[0, 0])
    slot_index = jnp.arange(block_ids.shape[-1], dtype=jnp.int32)
    for round_index in range(block_ids.shape[2]):
        listed = block_ids[0, 0, round_index]
        in_use = slot_index < block_counts[0, 0, round_index]
        packed = jnp.where(in_use[:, None, None], current[listed] - public_blocks[listed], 0.0)
        public_blocks = public_blocks.at[listed].add(packed)
        mixed_blocks = mixed_blocks.at[listed].add(NEIGHBOUR_WEIGHT * packed)
        from_west = shifted((packed, listed), "wide", 1)
        from_east = shifted((packed, listed), "wide", -1)
        from_north = shifted((packed, listed), "narrow", 1)
        from_south = shifted((packed, listed), "narrow", -1)
        for arrived in (from_west, from_east, from_north, from_south):
            mixed_blocks = mixed_blocks.at[arrived[1]].add(NEIGHBOUR_WEIGHT * arrived[0])
        current = current + CONSENSUS * (mixed_blocks - public_blocks)
    return (from_blocks(current), from_blocks(public_blocks), from_blocks(mixed_blocks))


def solution(mesh):
    in_specs = (
        P("wide", "narrow", None, None),
        P("wide", "narrow", None, None),
        P("wide", "narrow", None, None),
        P("wide", "narrow", None, None),
        P("wide", "narrow", None, None),
        P("wide", "narrow", None, None),
        P("wide", "narrow", None),
    )
    out_specs = (
        P("wide", "narrow", None, None),
        P("wide", "narrow", None, None),
        P("wide", "narrow", None, None),
    )
    return jax.shard_map(
        on_device, mesh=mesh, in_specs=in_specs, out_specs=out_specs, check_vma=False
    )
```

profile of v0, /device:TPU:0, one launch (start us, length us, event | category | flops | bytes accessed | tf_op | source)
XLA Modules:
  0.0 135.1 jit_solution(14816248491773806564)
XLA Ops:
  1.9 2.9 %collective-permute-start.2 = (s32[8]{0:T(128)S(1)}, s32[8]{0:T(128)S(1)}, u32[]{:S(2)}, u32[]{:S(2)}) collective-permute-start(s32[8]{0:T(128)S(1)} %get-tuple-element.11), channel_id=1, source_target_pairs={{0,28},{4,0},{8,4},{12,8},{16,12},{20,16},{24,20},{28,24},{1,29},{... | collective-permute-start | bytes 104 | tf_op jit(solution)/shard_map/ppermute | solution.py:19
  5.5 3.5 %bitcast_subtract_fusion = f32[1024,512]{1,0:T(8,128)} fusion(f32[1,1,1024,512]{3,2,1,0:T(8,128)} %param.7, bf16[1,1,256,1024]{3,2,1,0:T(8,128)(2,1)S(1)} %copy-done, bf16[1,1,256,512]{3,2,1,0:T(8,128)(2,1)} %param.11), kind=kOutput, calls=%fused_computation.16 | convolution fusion | flops 269484032 | bytes 4980736 | tf_op jit(solution)/shard_map/dot_general | solution.py:39
  12.5 2.9 %reshape.247 = f32[8,128,4,128]{3,2,1,0:T(4,128)} reshape(f32[1,1,1024,512]{3,2,1,0:T(8,128)} %param.8) | data formatting | bytes 4194304 | tf_op jit(solution)/shard_map/reshape;squeeze | solution.py:25
  17.3 3.0 %gather_fusion = f32[8,128,128]{2,1,0:T(8,128)} fusion(f32[32,128,128]{2,1,0:T(8,128)} %bitcast.52, s32[1024]{0:T(1024)S(1)} %get-tuple-element.17), kind=kCustom, calls=%fused_computation | custom fusion | bytes 1048608 | tf_op jit(solution)/shard_map/gather | solution.py:49
  23.0 2.2 %broadcast_multiply_fusion.9 = (f32[8,128,128]{2,1,0:T(8,128)}, f32[8,128,128]{2,1,0:T(8,128)S(1)}) fusion(f32[8,128,128]{2,1,0:T(8,128)} %gather_fusion, f32[8,128,128]{2,1,0:T(8,128)} %gather_fusion.1, pred[8]{0:T(512)(128)(4,1)S(1)} %iota_compare_fusion.1), kind=kLoop, calls=%fused_computation.32 | loop fusion | flops 393216 | bytes 2097160 | tf_op jit(solution)/shard_map/mul | solution.py:51
  25.2 2.6 %collective-permute-start.3 = (f32[8,128,128]{2,1,0:T(8,128)S(1)}, f32[8,128,128]{2,1,0:T(8,128)}, u32[]{:S(2)}, u32[]{:S(2)}) collective-permute-start(f32[8,128,128]{2,1,0:T(8,128)S(1)} %get-tuple-element.9), channel_id=1, source_target_pairs={{0,28},{4,0},{8,4},{12,8},{16,12},{20,16},{24,20},{28,24},{1,29},{... | collective-permute-start | bytes 1572872 | tf_op jit(solution)/shard_map/ppermute | solution.py:19
  27.8 2.3 %collective-permute-start.4 = (s32[8]{0:T(128)S(1)}, s32[8]{0:T(128)S(1)}, u32[]{:S(2)}, u32[]{:S(2)}) collective-permute-start(s32[8]{0:T(128)S(1)} %get-tuple-element.11), channel_id=1, source_target_pairs={{0,1},{1,2},{2,3},{3,0},{4,5},{5,6},{6,7},{7,4},{8,9},{9,10},{10,1... | collective-permute-start | bytes 104 | tf_op jit(solution)/shard_map/ppermute | solution.py:19
  32.5 2.9 %reshape.246 = f32[8,128,4,128]{3,2,1,0:T(4,128)} reshape(f32[1,1,1024,512]{3,2,1,0:T(8,128)} %param.9) | data formatting | bytes 4194304 | tf_op jit(solution)/shard_map/reshape;squeeze | solution.py:25
  37.9 2.0 %scatter_fusion = f32[32,128,128]{2,1,0:T(8,128)S(1)} fusion(f32[32,128,128]{2,1,0:T(8,128)S(1)} %bitcast.47, s32[8]{0:T(128)S(1)} %get-tuple-element.13, f32[8,128,128]{2,1,0:T(8,128)} %get-tuple-element.8), kind=kCustom, calls=%fused_computation.4 | custom fusion | flops 131072 | bytes 1572896 | tf_op jit(solution)/shard_map/scatter-add | solution.py:51
  39.9 3.0 %gather_fusion.3 = f32[8,128,128]{2,1,0:T(8,128)} fusion(f32[32,128,128]{2,1,0:T(8,128)} %copy-done.1, s32[1024]{0:T(1024)S(1)} %get-tuple-element.16), kind=kCustom, calls=%fused_computation.3 | custom fusion | bytes 1048608 | tf_op jit(solution)/shard_map/gather | solution.py:49
  44.5 2.2 %collective-permute-start.6 = (s32[8]{0:T(128)S(1)}, s32[8]{0:T(128)S(1)}, u32[]{:S(2)}, u32[]{:S(2)}) collective-permute-start(s32[8]{0:T(128)S(1)} %get-tuple-element.11), channel_id=1, source_target_pairs={{0,3},{1,0},{2,1},{3,2},{4,7},{5,4},{6,5},{7,6},{8,11},{9,8},{10,9... | collective-permute-start | bytes 104 | tf_op jit(solution)/shard_map/ppermute | solution.py:19
  47.1 9.9 %collective-permute-done.6 = s32[8]{0:T(128)S(1)} collective-permute-done((s32[8]{0:T(128)S(1)}, s32[8]{0:T(128)S(1)}, u32[]{:S(2)}, u32[]{:S(2)}) %collective-permute-start.6) | collective-permute-done | bytes 64 | tf_op jit(solution)/shard_map/ppermute | solution.py:19
  56.9 3.9 %collective-permute-done.8 = s32[8]{0:T(128)S(1)} collective-permute-done((s32[8]{0:T(128)S(1)}, s32[8]{0:T(128)S(1)}, u32[]{:S(2)}, u32[]{:S(2)}) %collective-permute-start.8) | collective-permute-done | bytes 64 | tf_op jit(solution)/shard_map/ppermute | solution.py:19
  62.8 2.0 %scatter_fusion.1 = f32[32,128,128]{2,1,0:T(8,128)S(1)} fusion(f32[32,128,128]{2,1,0:T(8,128)S(1)} %scatter_fusion, s32[8]{0:T(128)S(1)} %compare_select_fusion.8, f32[8,128,128]{2,1,0:T(8,128)} %broadcast_multiply_fusion.8), kind=kCustom, calls=%fused_computation.5 | custom fusion | flops 131072 | bytes 1572896 | tf_op jit(solution)/shard_map/scatter-add | solution.py:57
  64.8 4.3 %collective-permute-start.14 = (s32[8]{0:T(128)S(1)}, s32[8]{0:T(128)S(1)}, u32[]{:S(2)}, u32[]{:S(2)}) collective-permute-start(s32[8]{0:T(128)S(1)} %get-tuple-element.10), channel_id=1, source_target_pairs={{0,3},{1,0},{2,1},{3,2},{4,7},{5,4},{6,5},{7,6},{8,11},{9,8},{10,9... | collective-permute-start | bytes 104 | tf_op jit(solution)/shard_map/ppermute | solution.py:19
  71.0 2.0 %scatter_fusion.2 = f32[32,128,128]{2,1,0:T(8,128)S(1)} fusion(f32[32,128,128]{2,1,0:T(8,128)S(1)} %scatter_fusion.1, s32[8]{0:T(128)S(1)} %compare_select_fusion.7, f32[8,128,128]{2,1,0:T(8,128)} %broadcast_multiply_fusion.7), kind=kCustom, calls=%fused_computation.6 | custom fusion | flops 131072 | bytes 1572896 | tf_op jit(solution)/shard_map/scatter-add | solution.py:57
  74.9 2.0 %scatter_fusion.3 = f32[32,128,128]{2,1,0:T(8,128)S(1)} fusion(f32[32,128,128]{2,1,0:T(8,128)S(1)} %scatter_fusion.2, s32[8]{0:T(128)S(1)} %compare_select_fusion.6, f32[8,128,128]{2,1,0:T(8,128)} %broadcast_multiply_fusion.6), kind=kCustom, calls=%fused_computation.7 | custom fusion | flops 131072 | bytes 1572896 | tf_op jit(solution)/shard_map/scatter-add | solution.py:57
  79.1 4.2 %multiply_add_fusion.1 = f32[32,128,128]{2,1,0:T(8,128)} fusion(f32[32,128,128]{2,1,0:T(8,128)S(1)} %scatter_fusion.4, f32[32,128,128]{2,1,0:T(8,128)} %copy-done.1, f32[8,128,4,128]{3,1,2,0:T(8,128)} %copy.11), kind=kLoop, calls=%fused_computation.18 | loop fusion | flops 1572864 | bytes 8388608 | tf_op jit(solution)/shard_map/add | solution.py:58
  83.3 3.0 %gather_fusion.2 = f32[8,128,128]{2,1,0:T(8,128)} fusion(f32[32,128,128]{2,1,0:T(8,128)} %multiply_add_fusion.1, s32[1024]{0:T(1024)S(1)} %get-tuple-element.16), kind=kCustom, calls=%fused_computation.2 | custom fusion | bytes 1048608 | tf_op jit(solution)/shard_map/gather | solution.py:49
  86.3 2.2 %broadcast_multiply_fusion.4 = (f32[8,128,128]{2,1,0:T(8,128)}, f32[8,128,128]{2,1,0:T(8,128)S(1)}) fusion(f32[8,128,128]{2,1,0:T(8,128)} %gather_fusion.2, f32[8,128,128]{2,1,0:T(8,128)} %gather_fusion.3, pred[8]{0:T(512)(128)(4,1)S(1)} %iota_compare_fusion), kind=kLoop, calls=%fused_computation.27 | loop fusion | flops 393216 | bytes 2097160 | tf_op jit(solution)/shard_map/mul | solution.py:51
  88.6 2.5 %collective-permute-start.11 = (f32[8,128,128]{2,1,0:T(8,128)S(1)}, f32[8,128,128]{2,1,0:T(8,128)}, u32[]{:S(2)}, u32[]{:S(2)}) collective-permute-start(f32[8,128,128]{2,1,0:T(8,128)S(1)} %get-tuple-element.7), channel_id=1, source_target_pairs={{0,28},{4,0},{8,4},{12,8},{16,12},{20,16},{24,20},{28,24},{1,29},{... | collective-permute-start | bytes 1572872 | tf_op jit(solution)/shard_map/ppermute | solution.py:19
  91.1 3.8 %collective-permute-start.15 = (f32[8,128,128]{2,1,0:T(8,128)S(1)}, f32[8,128,128]{2,1,0:T(8,128)}, u32[]{:S(2)}, u32[]{:S(2)}) collective-permute-start(f32[8,128,128]{2,1,0:T(8,128)S(1)} %get-tuple-element.7), channel_id=1, source_target_pairs={{0,3},{1,0},{2,1},{3,2},{4,7},{5,4},{6,5},{7,6},{8,11},{9,8},{10,9... | collective-permute-start | bytes 1572872 | tf_op jit(solution)/shard_map/ppermute | solution.py:19
  94.9 2.7 %scatter_fusion.11 = f32[32,128,128]{2,1,0:T(8,128)} fusion(f32[32,128,128]{2,1,0:T(8,128)} %copy-done.1, s32[8]{0:T(128)S(1)} %get-tuple-element.12, f32[8,128,128]{2,1,0:T(8,128)S(1)} %get-tuple-element.7), kind=kCustom, calls=%fused_computation.15 | custom fusion | flops 131072 | bytes 1572896 | tf_op jit(solution)/shard_map/scatter-add | solution.py:50
  97.6 2.0 %scatter_fusion.6 = f32[32,128,128]{2,1,0:T(8,128)S(1)} fusion(f32[32,128,128]{2,1,0:T(8,128)S(1)} %scatter_fusion.4, s32[8]{0:T(128)S(1)} %get-tuple-element.12, f32[8,128,128]{2,1,0:T(8,128)} %get-tuple-element.6), kind=kCustom, calls=%fused_computation.10 | custom fusion | flops 131072 | bytes 1572896 | tf_op jit(solution)/shard_map/scatter-add | solution.py:51
  99.6 4.3 %copy.27 = f32[8,128,4,128]{3,2,1,0:T(4,128)} copy(f32[8,128,4,128]{3,1,2,0:T(8,128)} %bitcast.51) | data formatting | bytes 4194304
  103.9 3.0 %reshape.249 = f32[1,1,1024,512]{3,2,1,0:T(8,128)} reshape(f32[8,128,4,128]{3,2,1,0:T(4,128)} %copy.27) | data formatting | bytes 4194304
  108.9 2.0 %scatter_fusion.7 = f32[32,128,128]{2,1,0:T(8,128)S(1)} fusion(f32[32,128,128]{2,1,0:T(8,128)S(1)} %scatter_fusion.6, s32[8]{0:T(128)S(1)} %compare_select_fusion.3, f32[8,128,128]{2,1,0:T(8,128)} %broadcast_multiply_fusion.3), kind=kCustom, calls=%fused_computation.11 | custom fusion | flops 131072 | bytes 1572896 | tf_op jit(solution)/shard_map/scatter-add | solution.py:57
  120.9 2.8 %multiply_add_fusion = f32[32,128,128]{2,1,0:T(8,128)S(1)} fusion(f32[32,128,128]{2,1,0:T(8,128)} %multiply_add_fusion.1, f32[32,128,128]{2,1,0:T(8,128)S(1)} %scatter_fusion.10, f32[32,128,128]{2,1,0:T(8,128)} %scatter_fusion.11), kind=kLoop, calls=%fused_computation.17 | loop fusion | flops 1572864 | bytes 8388608 | tf_op jit(solution)/shard_map/add | solution.py:58
  123.7 2.7 %copy.26 = f32[8,128,4,128]{3,2,1,0:T(4,128)} copy(f32[8,128,4,128]{3,1,2,0:T(8,128)S(1)} %bitcast.53) | data formatting | bytes 4194304
  126.3 3.0 %reshape.248 = f32[1,1,1024,512]{3,2,1,0:T(8,128)} reshape(f32[8,128,4,128]{3,2,1,0:T(4,128)} %copy.26) | data formatting | bytes 4194304
  129.4 2.7 %copy.28 = f32[8,128,4,128]{3,2,1,0:T(4,128)} copy(f32[8,128,4,128]{3,1,2,0:T(8,128)S(1)} %bitcast.48) | data formatting | bytes 4194304
  132.1 3.0 %reshape.250 = f32[1,1,1024,512]{3,2,1,0:T(8,128)} reshape(f32[8,128,4,128]{3,2,1,0:T(4,128)} %copy.28) | data formatting | bytes 4194304
  (61 shorter events, 36.6 us)
Async XLA Ops:
  0.6 4.9 %copy-start = (bf16[1,1,256,1024]{3,2,1,0:T(8,128)(2,1)S(1)}, bf16[1,1,256,1024]{3,2,1,0:T(8,128)(2,1)}, u32[]{:S(2)}) copy-start(bf16[1,1,256,1024]{3,2,1,0:T(8,128)(2,1)} %param.10) | copy-start | bytes 1572868
  1.4 41.5 %collective-permute-start = (s32[8]{0:T(128)S(1)}, s32[8]{0:T(128)S(1)}, u32[]{:S(2)}, u32[]{:S(2)}) collective-permute-start(s32[8]{0:T(128)S(1)} %get-tuple-element.11), channel_id=1, source_target_pairs={{0,4},{4,8},{8,12},{12,16},{16,20},{20,24},{24,28},{28,0},{1,5},{5... | collective-permute-start | bytes 104 | tf_op jit(solution)/shard_map/ppermute | solution.py:19
  1.9 42.6 %collective-permute-start.2 = (s32[8]{0:T(128)S(1)}, s32[8]{0:T(128)S(1)}, u32[]{:S(2)}, u32[]{:S(2)}) collective-permute-start(s32[8]{0:T(128)S(1)} %get-tuple-element.11), channel_id=1, source_target_pairs={{0,28},{4,0},{8,4},{12,8},{16,12},{20,16},{24,20},{28,24},{1,29},{... | collective-permute-start | bytes 104 | tf_op jit(solution)/shard_map/ppermute | solution.py:19
  17.3 4.4 %copy-start.2 = (s32[1,1,2]{2,1,0:T(1,128)S(1)}, s32[1,1,2]{2,1,0:T(1,128)}, u32[]{:S(2)}) copy-start(s32[1,1,2]{2,1,0:T(1,128)} %param.13) | copy-start | bytes 28
  25.2 35.6 %collective-permute-start.1 = (f32[8,128,128]{2,1,0:T(8,128)S(1)}, f32[8,128,128]{2,1,0:T(8,128)}, u32[]{:S(2)}, u32[]{:S(2)}) collective-permute-start(f32[8,128,128]{2,1,0:T(8,128)S(1)} %get-tuple-element.9), channel_id=1, source_target_pairs={{0,4},{4,8},{8,12},{12,16},{16,20},{20,24},{24,28},{28,0},{1,5},{5... | collective-permute-start | bytes 1572872 | tf_op jit(solution)/shard_map/ppermute | solution.py:19
  25.2 39.6 %collective-permute-start.3 = (f32[8,128,128]{2,1,0:T(8,128)S(1)}, f32[8,128,128]{2,1,0:T(8,128)}, u32[]{:S(2)}, u32[]{:S(2)}) collective-permute-start(f32[8,128,128]{2,1,0:T(8,128)S(1)} %get-tuple-element.9), channel_id=1, source_target_pairs={{0,28},{4,0},{8,4},{12,8},{16,12},{20,16},{24,20},{28,24},{1,29},{... | collective-permute-start | bytes 1572872 | tf_op jit(solution)/shard_map/ppermute | solution.py:19
  27.8 18.9 %collective-permute-start.4 = (s32[8]{0:T(128)S(1)}, s32[8]{0:T(128)S(1)}, u32[]{:S(2)}, u32[]{:S(2)}) collective-permute-start(s32[8]{0:T(128)S(1)} %get-tuple-element.11), channel_id=1, source_target_pairs={{0,1},{1,2},{2,3},{3,0},{4,5},{5,6},{6,7},{7,4},{8,9},{9,10},{10,1... | collective-permute-start | bytes 104 | tf_op jit(solution)/shard_map/ppermute | solution.py:19
  31.2 1.3 copy-start.1
  42.9 30.1 %collective-permute-start.5 = (f32[8,128,128]{2,1,0:T(8,128)S(1)}, f32[8,128,128]{2,1,0:T(8,128)}, u32[]{:S(2)}, u32[]{:S(2)}) collective-permute-start(f32[8,128,128]{2,1,0:T(8,128)S(1)} %get-tuple-element.9), channel_id=1, source_target_pairs={{0,1},{1,2},{2,3},{3,0},{4,5},{5,6},{6,7},{7,4},{8,9},{9,10},{10,1... | collective-permute-start | bytes 1572872 | tf_op jit(solution)/shard_map/ppermute | solution.py:19
  44.5 12.4 %collective-permute-start.6 = (s32[8]{0:T(128)S(1)}, s32[8]{0:T(128)S(1)}, u32[]{:S(2)}, u32[]{:S(2)}) collective-permute-start(s32[8]{0:T(128)S(1)} %get-tuple-element.11), channel_id=1, source_target_pairs={{0,3},{1,0},{2,1},{3,2},{4,7},{5,4},{6,5},{7,6},{8,11},{9,8},{10,9... | collective-permute-start | bytes 104 | tf_op jit(solution)/shard_map/ppermute | solution.py:19
  46.8 30.1 %collective-permute-start.7 = (f32[8,128,128]{2,1,0:T(8,128)S(1)}, f32[8,128,128]{2,1,0:T(8,128)}, u32[]{:S(2)}, u32[]{:S(2)}) collective-permute-start(f32[8,128,128]{2,1,0:T(8,128)S(1)} %get-tuple-element.9), channel_id=1, source_target_pairs={{0,3},{1,0},{2,1},{3,2},{4,7},{5,4},{6,5},{7,6},{8,11},{9,8},{10,9... | collective-permute-start | bytes 1572872 | tf_op jit(solution)/shard_map/ppermute | solution.py:19
  56.9 3.9 %collective-permute-start.8 = (s32[8]{0:T(128)S(1)}, s32[8]{0:T(128)S(1)}, u32[]{:S(2)}, u32[]{:S(2)}) collective-permute-start(s32[8]{0:T(128)S(1)} %get-tuple-element.10), channel_id=1, source_target_pairs={{0,4},{4,8},{8,12},{12,16},{16,20},{20,24},{24,28},{28,0},{1,5},{5... | collective-permute-start | bytes 104 | tf_op jit(solution)/shard_map/ppermute | solution.py:19
  60.8 27.8 %collective-permute-start.10 = (s32[8]{0:T(128)S(1)}, s32[8]{0:T(128)S(1)}, u32[]{:S(2)}, u32[]{:S(2)}) collective-permute-start(s32[8]{0:T(128)S(1)} %get-tuple-element.10), channel_id=1, source_target_pairs={{0,28},{4,0},{8,4},{12,8},{16,12},{20,16},{24,20},{28,24},{1,29},{... | collective-permute-start | bytes 104 | tf_op jit(solution)/shard_map/ppermute | solution.py:19
  60.8 30.3 %collective-permute-start.12 = (s32[8]{0:T(128)S(1)}, s32[8]{0:T(128)S(1)}, u32[]{:S(2)}, u32[]{:S(2)}) collective-permute-start(s32[8]{0:T(128)S(1)} %get-tuple-element.10), channel_id=1, source_target_pairs={{0,1},{1,2},{2,3},{3,0},{4,5},{5,6},{6,7},{7,4},{8,9},{9,10},{10,1... | collective-permute-start | bytes 104 | tf_op jit(solution)/shard_map/ppermute | solution.py:19
  64.8 26.3 %collective-permute-start.14 = (s32[8]{0:T(128)S(1)}, s32[8]{0:T(128)S(1)}, u32[]{:S(2)}, u32[]{:S(2)}) collective-permute-start(s32[8]{0:T(128)S(1)} %get-tuple-element.10), channel_id=1, source_target_pairs={{0,3},{1,0},{2,1},{3,2},{4,7},{5,4},{6,5},{7,6},{8,11},{9,8},{10,9... | collective-permute-start | bytes 104 | tf_op jit(solution)/shard_map/ppermute | solution.py:19
  88.4 18.5 %collective-permute-start.9 = (f32[8,128,128]{2,1,0:T(8,128)S(1)}, f32[8,128,128]{2,1,0:T(8,128)}, u32[]{:S(2)}, u32[]{:S(2)}) collective-permute-start(f32[8,128,128]{2,1,0:T(8,128)S(1)} %get-tuple-element.7), channel_id=1, source_target_pairs={{0,4},{4,8},{8,12},{12,16},{16,20},{20,24},{24,28},{28,0},{1,5},{5... | collective-permute-start | bytes 1572872 | tf_op jit(solution)/shard_map/ppermute | solution.py:19
  88.6 22.3 %collective-permute-start.11 = (f32[8,128,128]{2,1,0:T(8,128)S(1)}, f32[8,128,128]{2,1,0:T(8,128)}, u32[]{:S(2)}, u32[]{:S(2)}) collective-permute-start(f32[8,128,128]{2,1,0:T(8,128)S(1)} %get-tuple-element.7), channel_id=1, source_target_pairs={{0,28},{4,0},{8,4},{12,8},{16,12},{20,16},{24,20},{28,24},{1,29},{... | collective-permute-start | bytes 1572872 | tf_op jit(solution)/shard_map/ppermute | solution.py:19
  91.1 23.7 %collective-permute-start.13 = (f32[8,128,128]{2,1,0:T(8,128)S(1)}, f32[8,128,128]{2,1,0:T(8,128)}, u32[]{:S(2)}, u32[]{:S(2)}) collective-permute-start(f32[8,128,128]{2,1,0:T(8,128)S(1)} %get-tuple-element.7), channel_id=1, source_target_pairs={{0,1},{1,2},{2,3},{3,0},{4,5},{5,6},{6,7},{7,4},{8,9},{9,10},{10,1... | collective-permute-start | bytes 1572872 | tf_op jit(solution)/shard_map/ppermute | solution.py:19
  91.1 27.6 %collective-permute-start.15 = (f32[8,128,128]{2,1,0:T(8,128)S(1)}, f32[8,128,128]{2,1,0:T(8,128)}, u32[]{:S(2)}, u32[]{:S(2)}) collective-permute-start(f32[8,128,128]{2,1,0:T(8,128)S(1)} %get-tuple-element.7), channel_id=1, source_target_pairs={{0,3},{1,0},{2,1},{3,2},{4,7},{5,4},{6,5},{7,6},{8,11},{9,8},{10,9... | collective-permute-start | bytes 1572872 | tf_op jit(solution)/shard_map/ppermute | solution.py:19
where the time goes:
time: 137 us; the launch traced here: 135 us
  other arithmetic  48.9 us (36%)
  local copies, waits for them, and re-layouts  44.8 us (33%)
  starting transfers between devices  23.2 us (17%)
  waiting for transfers between devices  13.8 us (10%)
  matrix products  3.48 us (3%)
    ppermute x16, starting transfers between devices, shifted(): return lax.ppermute(value, axis, pairs)  23.2 us
    unnamed x12, local copies, waits for them, and re-layouts  20.1 us
    scatter-add x8, other arithmetic, on_device(): mixed_blocks.at[arrived[1]].add(NEIGHBOUR_WEIGHT * arrived[0])  14.2 us
    ppermute x16, waiting for transfers between devices, shifted(): return lax.ppermute(value, axis, pairs)  13.8 us
    mul x8, other arithmetic, on_device(): NEIGHBOUR_WEIGHT * arrived[0]  13.5 us
    add x2, other arithmetic, on_device(): current = current + CONSENSUS * (mixed_blocks - public_blocks)  7.01 us
    gather x2, local copies, waits for them, and re-layouts, on_device(): current[listed] - public_blocks[listed]  5.93 us
    another operation x2, local copies, waits for them, and re-layouts, to_blocks(): shaped = matrix.reshape(row_tiles, TILE, col_tiles, TILE)  5.77 us
  transfers between devices with their start and end apart: 16, of which 2 were waited for; matrix products, arithmetic and copies ran while one was open for 58% of the time, Pallas kernels for 0%

commit v1 on v0

v1 whole, which is shorter than its diff:
```python
import functools

import jax
import jax.numpy as jnp
from jax import lax
from jax.experimental import pallas as pl
from jax.experimental.pallas import tpu as pltpu
from jax.sharding import PartitionSpec as P

TILE = 128
LEARN_RATE = 0.05
NEIGHBOUR_WEIGHT = 0.2
CONSENSUS = 0.4
CHUNK = 256
SUBLANES = 8
SIDES = 4
MESH = pl.DeviceIdType.MESH


def kernel(
    sizes, rounds, slots, ids, bands, columns, counts, params, public, mixed, inputs, cotangent,
    params_out, public_out, mixed_out,
    acts, cots, cur, pub, mix, maps, map_table, load_sem, map_send, map_recv, table_sem,
    send_sem, recv_sem, out_sem, *buffers
):
    sends, recvs = buffers[:rounds], buffers[rounds:]
    row_tiles, col_tiles = cur.shape[:2]
    rows = row_tiles * TILE
    wide, narrow = lax.axis_index("wide"), lax.axis_index("narrow")
    wide_size, narrow_size = sizes
    partners = (
        (wide, lax.rem(narrow + 1, narrow_size)),
        (wide, lax.rem(narrow + narrow_size - 1, narrow_size)),
        (lax.rem(wide + 1, wide_size), narrow),
        (lax.rem(wide + wide_size - 1, wide_size), narrow),
    )

    load_acts = pltpu.make_async_copy(inputs.at[0, 0], acts, load_sem.at[0])
    load_cots = pltpu.make_async_copy(cotangent.at[0, 0], cots, load_sem.at[1])

    def column_loads(source, held, first):
        return [
            pltpu.make_async_copy(
                source.at[:, :, pl.ds(j * TILE, TILE)], held.at[:, j], load_sem.at[first + j]
            )
            for j in range(col_tiles)
        ]

    load_cur = column_loads(params, cur, 2)
    load_pub = column_loads(public, pub, 2 + col_tiles)
    load_mix = column_loads(mixed, mix, 2 + 2 * col_tiles)
    for load in [load_acts, load_cots] + load_cur + load_pub + load_mix:
        load.start()

    barrier = pltpu.get_barrier_semaphore()
    for partner in partners:
        pl.semaphore_signal(barrier, inc=1, device_id=partner, device_id_type=MESH)

    row = lax.broadcasted_iota(jnp.int32, (SUBLANES, TILE), 0)
    lane = lax.broadcasted_iota(jnp.int32, (SUBLANES, TILE), 1)
    own_map = jnp.full((SUBLANES, TILE), slots, jnp.int32)
    for r in range(rounds):
        for s in range(slots):
            used = jnp.full((SUBLANES, TILE), counts[r], jnp.int32) > s
            own_map = jnp.where((row == r) & (lane == ids[r, s]) & used, s, own_map)
    maps[0] = own_map
    for r in range(rounds):
        sends[r][slots] = jnp.zeros((TILE, TILE), jnp.float32)
        for side in range(SIDES):
            recvs[r][side, slots] = jnp.zeros((TILE, TILE), jnp.float32)

    pl.semaphore_wait(barrier, SIDES)
    map_copies = [
        pltpu.make_async_remote_copy(
            src_ref=maps.at[0], dst_ref=maps.at[1 + side], send_sem=map_send.at[side],
            recv_sem=map_recv.at[side], device_id=partners[side], device_id_type=MESH,
        )
        for side in range(SIDES)
    ]
    for copy in map_copies:
        copy.start()

    def slot_copy(r, side, first, size):
        return pltpu.make_async_remote_copy(
            src_ref=sends[r].at[pl.ds(first, size)],
            dst_ref=recvs[r].at[side, pl.ds(first, size)],
            send_sem=send_sem.at[r, side], recv_sem=recv_sem.at[r, side],
            device_id=partners[side], device_id_type=MESH,
        )

    def arrived(r, tile):
        total = recvs[r][0, map_table[1, r, tile]]
        for side in range(1, SIDES):
            total = total + recvs[r][side, map_table[1 + side, r, tile]]
        return total

    load_acts.wait()
    load_cots.wait()
    for load in load_cur:
        load.wait()
    for first in range(0, rows, CHUNK):
        gradient = lax.dot_general(
            acts[:, first:first + CHUNK], cots[...], (((0,), (0,)), ((), ())),
            preferred_element_type=jnp.float32,
        )
        for j in range(col_tiles):
            for i in range(CHUNK // TILE):
                part = gradient[i * TILE:(i + 1) * TILE, j * TILE:(j + 1) * TILE]
                at = first // TILE + i
                cur[at, j] = cur[at, j] - LEARN_RATE * part
    for load in load_pub:
        load.wait()

    for r in range(rounds):
        for s in range(slots):
            tile = ids[r, s]
            i, j = bands[r, s], columns[r, s]
            value = cur[i, j]
            if r:
                value = value + CONSENSUS * NEIGHBOUR_WEIGHT * arrived(r - 1, tile)
            sends[r][s] = value - pub[i, j]
            for side in range(SIDES):
                slot_copy(r, side, s, 1).start()

        if r == 0:
            for copy in map_copies:
                copy.wait()
            table = pltpu.make_async_copy(maps, map_table, table_sem)
            table.start()
            table.wait()
            for load in load_mix:
                load.wait()

        for j in range(col_tiles):
            def own_part(i, carry):
                tile = i * col_tiles + j
                q = sends[r][map_table[0, r, tile]]
                new_pub = pub[i, j] + q
                new_cur, new_mix = cur[i, j], mix[i, j]
                if r:
                    total = arrived(r - 1, tile)
                    new_cur = new_cur + CONSENSUS * NEIGHBOUR_WEIGHT * total
                    q = q + total
                new_mix = new_mix + NEIGHBOUR_WEIGHT * q
                pub[i, j] = new_pub
                mix[i, j] = new_mix
                cur[i, j] = new_cur + CONSENSUS * (new_mix - new_pub)
                return carry

            lax.fori_loop(0, row_tiles, own_part, 0)

        if r == rounds - 1:
            writes = [
                pltpu.make_async_copy(
                    pub.at[:, j], public_out.at[:, :, pl.ds(j * TILE, TILE)], out_sem.at[j]
                )
                for j in range(col_tiles)
            ]
            for write in writes:
                write.start()
        for side in range(SIDES):
            slot_copy(r, side, 0, slots).wait_recv()

    last = rounds - 1
    for j in range(col_tiles):
        def last_part(i, carry):
            total = arrived(last, i * col_tiles + j)
            mix[i, j] = mix[i, j] + NEIGHBOUR_WEIGHT * total
            cur[i, j] = cur[i, j] + CONSENSUS * NEIGHBOUR_WEIGHT * total
            return carry

        lax.fori_loop(0, row_tiles, last_part, 0)
        for place, (held, target) in enumerate(((cur, params_out), (mix, mixed_out))):
            write = pltpu.make_async_copy(
                held.at[:, j], target.at[:, :, pl.ds(j * TILE, TILE)],
                out_sem.at[(1 + place) * col_tiles + j],
            )
            write.start()
            writes.append(write)
    for r in range(rounds):
        for side in range(SIDES):
            slot_copy(r, side, 0, slots).wait_send()
    for write in writes:
        write.wait()


def solution(mesh):
    sizes = (mesh.shape["wide"], mesh.shape["narrow"])

    def on_device(params, public, mixed, inputs, cotangent, block_ids, block_counts):
        rounds, slots = block_ids.shape[2:]
        rows, cols = params.shape[2:]
        tokens = inputs.shape[2]
        col_tiles = cols // TILE
        banded = (rows // TILE, TILE, cols)
        held = pltpu.VMEM((rows // TILE, col_tiles, TILE, TILE), jnp.float32)
        any_spec = pl.BlockSpec(memory_space=pl.ANY)
        smem_spec = pl.BlockSpec(memory_space=pltpu.SMEM)
        shape = jax.ShapeDtypeStruct(banded, jnp.float32)
        ids = block_ids.reshape(rounds, slots)
        outs = pl.pallas_call(
            functools.partial(kernel, sizes, rounds, slots),
            out_shape=(shape, shape, shape),
            in_specs=[smem_spec] * 4 + [any_spec] * 5,
            out_specs=(any_spec,) * 3,
            scratch_shapes=[
                pltpu.VMEM((tokens, rows), inputs.dtype),
                pltpu.VMEM((tokens, cols), cotangent.dtype),
                held, held, held,
                pltpu.VMEM((1 + SIDES, SUBLANES, TILE), jnp.int32),
                pltpu.SMEM((1 + SIDES, SUBLANES, TILE), jnp.int32),
                pltpu.SemaphoreType.DMA((2 + 3 * col_tiles,)),
                pltpu.SemaphoreType.DMA((SIDES,)),
                pltpu.SemaphoreType.DMA((SIDES,)),
                pltpu.SemaphoreType.DMA,
                pltpu.SemaphoreType.DMA((rounds, SIDES)),
                pltpu.SemaphoreType.DMA((rounds, SIDES)),
                pltpu.SemaphoreType.DMA((3 * col_tiles,)),
            ]
            + [pltpu.VMEM((slots + 1, TILE, TILE), jnp.float32)] * rounds
            + [pltpu.VMEM((SIDES, slots + 1, TILE, TILE), jnp.float32)] * rounds,
            compiler_params=pltpu.CompilerParams(
                collective_id=0, has_side_effects=True, vmem_limit_bytes=48 * 1024 * 1024
            ),
            cost_estimate=pl.CostEstimate(
                flops=2 * tokens * rows * cols, bytes_accessed=6 * 4 * rows * cols, transcendentals=0
            ),
        )(
            ids, ids // col_tiles, ids % col_tiles, block_counts.reshape(rounds),
            params.reshape(banded), public.reshape(banded), mixed.reshape(banded), inputs, cotangent,
        )
        return tuple(out.reshape(params.shape) for out in outs)

    spec = P("wide", "narrow", None, None)
    return jax.shard_map(
        on_device, mesh=mesh, in_specs=(spec,) * 6 + (P("wide", "narrow", None),),
        out_specs=(spec,) * 3, check_vma=False,
    )
```

time: 137 us -> 66.9 us (0.49); the launches traced: 135 us -> 66.6 us
  Pallas kernels: 0 us -> 57 us
  other arithmetic: 48.9 us -> 0.69 us
  local copies, waits for them, and re-layouts: 44.8 us -> 8.31 us
  starting transfers between devices: 23.2 us -> 0 us
  waiting for transfers between devices: 13.8 us -> 0 us
  matrix products: 3.48 us -> 0 us
    pallas_call x0 -> x1, Pallas kernels: none -> 57 us  [on_device(): pl.pallas_call(functools.partial(kernel, sizes, rounds, slots), out_shape...]
    ppermute x16 -> x0, starting transfers between devices: 23.2 us -> none  [shifted(): return lax.ppermute(value, axis, pairs)]
    scatter-add x12 -> x0, other arithmetic: 22 us -> none  [the longest x8 14.2 us: on_device(): mixed_blocks.at[arrived[1]].add(NEIGHBOUR_WEIGHT * arrived[0])]
    mul x10 -> x0, other arithmetic: 17.9 us -> none  [the longest x8 13.5 us: on_device(): NEIGHBOUR_WEIGHT * arrived[0]]
    ppermute x16 -> x0, waiting for transfers between devices: 13.8 us -> none  [shifted(): return lax.ppermute(value, axis, pairs)]
    unnamed x12 -> x13, local copies, waits for them, and re-layouts: 20.1 us -> 8.31 us
    gather x4 -> x0, local copies, waits for them, and re-layouts: 10.3 us -> none  [the longest x2 5.93 us: on_device(): current[listed] - public_blocks[listed]]
    add x2 -> x0, other arithmetic: 7.01 us -> none  [on_device(): current = current + CONSENSUS * (mixed_blocks - public_blocks)]
  transfers between devices with their start and end apart: 16 -> 0, of which waited for: 2 -> 0; matrix products, arithmetic and copies ran while one was open for 58% -> 0% of each run, Pallas kernels for 0% -> 0%
where the time goes in v1:
time: 66.9 us; the launch traced here: 66.6 us
  Pallas kernels  57 us (85%)
  local copies, waits for them, and re-layouts  8.31 us (12%)
  other arithmetic  0.69 us (1%)
    pallas_call x1, Pallas kernels, on_device(): pl.pallas_call(functools.partial(kernel, sizes, rounds, slots), out_shape...  57 us
    unnamed x13, local copies, waits for them, and re-layouts  8.31 us

profile of v1, /device:TPU:0, one launch (start us, length us, event | category | flops | bytes accessed | tf_op | source)
XLA Modules:
  0.0 66.6 jit_solution(8000498679993315765)
XLA Ops:
  0.6 0.7 %and_select_fusion = (s32[2,8]{1,0:T(2,128)S(1)}, s32[2,8]{1,0:T(2,128)S(1)}) fusion(s32[1,1,2,8]{3,2,1,0:T(2,128)} %param.12), kind=kLoop, calls=%fused_computation | loop fusion | flops 304 | bytes 192 | tf_op jit(solution)/shard_map/jit(remainder)/select_n | solution.py:229
  1.3 0.0 copy-start
  1.3 1.0 %copy-done = bf16[1,1,256,1024]{3,2,1,0:T(8,128)(2,1)S(1)} copy-done((bf16[1,1,256,1024]{3,2,1,0:T(8,128)(2,1)S(1)}, bf16[1,1,256,1024]{3,2,1,0:T(8,128)(2,1)}, u32[]{:S(2)}) %copy-start) | copy-done | bytes 524312
  2.4 0.0 copy-start.1
  2.4 0.9 %copy-done.1 = bf16[1,1,256,512]{3,2,1,0:T(8,128)(2,1)S(1)} copy-done((bf16[1,1,256,512]{3,2,1,0:T(8,128)(2,1)S(1)}, bf16[1,1,256,512]{3,2,1,0:T(8,128)(2,1)}, u32[]{:S(2)}) %copy-start.1) | copy-done | bytes 262168
  3.3 0.0 copy-start.2
  3.3 0.7 %copy-done.2 = s32[1,1,2,8]{3,2,1,0:T(2,128)S(1)} copy-done((s32[1,1,2,8]{3,2,1,0:T(2,128)S(1)}, s32[1,1,2,8]{3,2,1,0:T(2,128)}, u32[]{:S(2)}) %copy-start.2) | copy-done | bytes 88
  4.0 0.0 copy-start.3
  4.0 0.7 copy-done.3
  4.6 57.0 %shard_map.94 = (f32[8,128,512]{2,1,0:T(8,128)S(1)}, f32[8,128,512]{2,1,0:T(8,128)S(1)}, f32[8,128,512]{2,1,0:T(8,128)}) custom-call(s32[2,8]{1,0:T(2,128)S(1)} %bitcast.16, s32[2,8]{1,0:T(2,128)S(1)} %get-tuple-element.10.bands, s32[2,8]{1,0:T(2,128)S(1)} %get-tuple-element.9.columns, s32[2]{0:T(128)S(1)} %bitcast.17, f32[8,128,512]{2,1,0:T(8,128)} %bitcast.18, ...), custom_call_target="tpu_custom_call" | custom-call | flops 268435456 | bytes 12582912 | tf_op jit(solution)/shard_map/pallas_call | solution.py:201
  61.6 1.3 %copy.13 = f32[1,1,1024,512]{3,2,1,0:T(8,128)} copy(f32[1,1,1024,512]{3,2,1,0:T(8,128)S(1)} %bitcast.15) | data formatting | bytes 4194304
  63.0 0.0 copy-start.4
  63.0 1.3 %copy.14 = f32[1,1,1024,512]{3,2,1,0:T(8,128)} copy(f32[1,1,1024,512]{3,2,1,0:T(8,128)S(1)} %bitcast.14) | data formatting | bytes 4194304
  64.3 1.0 %copy-done.4 = f32[8,128,512]{2,1,0:T(8,128)S(1)} copy-done((f32[8,128,512]{2,1,0:T(8,128)S(1)}, f32[8,128,512]{2,1,0:T(8,128)}, u32[]{:S(2)}) %copy-start.4) | copy-done | bytes 2097176
  65.3 1.3 %copy.15 = f32[1,1,1024,512]{3,2,1,0:T(8,128)} copy(f32[1,1,1024,512]{3,2,1,0:T(8,128)S(1)} %bitcast.21) | data formatting | bytes 4194304
Async XLA Ops:
  1.3 1.0 %copy-start = (bf16[1,1,256,1024]{3,2,1,0:T(8,128)(2,1)S(1)}, bf16[1,1,256,1024]{3,2,1,0:T(8,128)(2,1)}, u32[]{:S(2)}) copy-start(bf16[1,1,256,1024]{3,2,1,0:T(8,128)(2,1)} %inputs.1) | copy-start | bytes 1572868
  2.4 0.9 %copy-start.1 = (bf16[1,1,256,512]{3,2,1,0:T(8,128)(2,1)S(1)}, bf16[1,1,256,512]{3,2,1,0:T(8,128)(2,1)}, u32[]{:S(2)}) copy-start(bf16[1,1,256,512]{3,2,1,0:T(8,128)(2,1)} %cotangent.1) | copy-start | bytes 786436
  3.3 0.7 %copy-start.2 = (s32[1,1,2,8]{3,2,1,0:T(2,128)S(1)}, s32[1,1,2,8]{3,2,1,0:T(2,128)}, u32[]{:S(2)}) copy-start(s32[1,1,2,8]{3,2,1,0:T(2,128)} %param.12) | copy-start | bytes 196
  4.0 0.7 copy-start.3
  63.0 2.3 %copy-start.4 = (f32[8,128,512]{2,1,0:T(8,128)S(1)}, f32[8,128,512]{2,1,0:T(8,128)}, u32[]{:S(2)}) copy-start(f32[8,128,512]{2,1,0:T(8,128)} %get-tuple-element.8) | copy-start | bytes 6291460

commit v2 on v1

--- a/solution.py
+++ b/solution.py
@@ -12,18 +12,24 @@
 NEIGHBOUR_WEIGHT = 0.2
 CONSENSUS = 0.4
 CHUNK = 256
+STEP_BANDS = 2
+LIMIT = 24 * 1024 * 1024
 SUBLANES = 8
 SIDES = 4
 MESH = pl.DeviceIdType.MESH
 
 
+def in_hbm(x):
+    return pltpu.with_memory_space_constraint(x, pltpu.HBM)
+
+
 def kernel(
-    sizes, rounds, slots, ids, bands, columns, counts, params, public, mixed, inputs, cotangent,
-    params_out, public_out, mixed_out,
-    acts, cots, cur, pub, mix, maps, map_table, load_sem, map_send, map_recv, table_sem,
+    sizes, rounds, slots, ids_in, counts_in, params, public, mixed, inputs, cotangent,
+    cur_out, pub_out, mix_out, maps_out, last_recv,
+    ids, counts, acts, cots, cur, pub, mix, places, maps, map_table, load_sem, map_send, map_recv, table_sem,
     send_sem, recv_sem, out_sem, *buffers
 ):
-    sends, recvs = buffers[:rounds], buffers[rounds:]
+    sends, recvs = buffers[:rounds], buffers[rounds:] + (last_recv,)
     row_tiles, col_tiles = cur.shape[:2]
     rows = row_tiles * TILE
     wide, narrow = lax.axis_index("wide"), lax.axis_index("narrow")
@@ -35,6 +41,10 @@
         (lax.rem(wide + wide_size - 1, wide_size), narrow),
     )
 
+    load_lists = [
+        pltpu.make_async_copy(ids_in, ids, load_sem.at[2 + 3 * col_tiles]),
+        pltpu.make_async_copy(counts_in, counts, load_sem.at[3 + 3 * col_tiles]),
+    ]
     load_acts = pltpu.make_async_copy(inputs.at[0, 0], acts, load_sem.at[0])
     load_cots = pltpu.make_async_copy(cotangent.at[0, 0], cots, load_sem.at[1])
 
@@ -49,7 +59,7 @@
     load_cur = column_loads(params, cur, 2)
     load_pub = column_loads(public, pub, 2 + col_tiles)
     load_mix = column_loads(mixed, mix, 2 + 2 * col_tiles)
-    for load in [load_acts, load_cots] + load_cur + load_pub + load_mix:
+    for load in load_lists + [load_acts, load_cots] + load_cur + load_pub + load_mix:
         load.start()
 
     barrier = pltpu.get_barrier_semaphore()
@@ -58,16 +68,23 @@
 
     row = lax.broadcasted_iota(jnp.int32, (SUBLANES, TILE), 0)
     lane = lax.broadcasted_iota(jnp.int32, (SUBLANES, TILE), 1)
+    for load in load_lists:
+        load.wait()
     own_map = jnp.full((SUBLANES, TILE), slots, jnp.int32)
     for r in range(rounds):
         for s in range(slots):
-            used = jnp.full((SUBLANES, TILE), counts[r], jnp.int32) > s
-            own_map = jnp.where((row == r) & (lane == ids[r, s]) & used, s, own_map)
+            used = jnp.full((SUBLANES, TILE), counts[0, 0, r], jnp.int32) > s
+            own_map = jnp.where((row == r) & (lane == ids[0, 0, r, s]) & used, s, own_map)
     maps[0] = own_map
     for r in range(rounds):
         sends[r][slots] = jnp.zeros((TILE, TILE), jnp.float32)
+    for r in range(rounds - 1):
         for side in range(SIDES):
             recvs[r][side, slots] = jnp.zeros((TILE, TILE), jnp.float32)
+
+    for tile in range(row_tiles * col_tiles):
+        places[0, tile] = tile // col_tiles
+        places[1, tile] = tile % col_tiles
 
     pl.semaphore_wait(barrier, SIDES)
     map_copies = [
@@ -113,8 +130,8 @@
 
     for r in range(rounds):
         for s in range(slots):
-            tile = ids[r, s]
-            i, j = bands[r, s], columns[r, s]
+            tile = ids[0, 0, r, s]
+            i, j = places[0, tile], places[1, tile]
             value = cur[i, j]
             if r:
                 value = value + CONSENSUS * NEIGHBOUR_WEIGHT * arrived(r - 1, tile)
@@ -151,37 +168,38 @@
 
         if r == rounds - 1:
             writes = [
-                pltpu.make_async_copy(
-                    pub.at[:, j], public_out.at[:, :, pl.ds(j * TILE, TILE)], out_sem.at[j]
+                pltpu.make_async_copy(held, target, out_sem.at[n])
+                for n, (held, target) in enumerate(
+                    ((cur, cur_out), (pub, pub_out), (mix, mix_out), (maps, maps_out))
                 )
-                for j in range(col_tiles)
             ]
             for write in writes:
                 write.start()
         for side in range(SIDES):
             slot_copy(r, side, 0, slots).wait_recv()
 
-    last = rounds - 1
-    for j in range(col_tiles):
-        def last_part(i, carry):
-            total = arrived(last, i * col_tiles + j)
-            mix[i, j] = mix[i, j] + NEIGHBOUR_WEIGHT * total
-            cur[i, j] = cur[i, j] + CONSENSUS * NEIGHBOUR_WEIGHT * total
-            return carry
-
-        lax.fori_loop(0, row_tiles, last_part, 0)
-        for place, (held, target) in enumerate(((cur, params_out), (mix, mixed_out))):
-            write = pltpu.make_async_copy(
-                held.at[:, j], target.at[:, :, pl.ds(j * TILE, TILE)],
-                out_sem.at[(1 + place) * col_tiles + j],
-            )
-            write.start()
-            writes.append(write)
     for r in range(rounds):
         for side in range(SIDES):
             slot_copy(r, side, 0, slots).wait_send()
     for write in writes:
         write.wait()
+
+
+def finish(last, table, cur, pub, mix, arrivals, params_out, public_out, mixed_out):
+    bands, col_tiles = cur.shape[:2]
+    slots = arrivals.shape[1]
+    for band in range(bands):
+        for j in range(col_tiles):
+            tile = (pl.program_id(0) * bands + band) * col_tiles + j
+            total = jnp.zeros((TILE, TILE), jnp.float32)
+            for side in range(SIDES):
+                slot = table[1 + side, last, tile]
+                part = arrivals[side, jnp.minimum(slot, slots - 1)]
+                total = total + jnp.where(slot < slots, part, 0.0)
+            at = (band, slice(None), slice(j * TILE, (j + 1) * TILE))
+            params_out[at] = cur[band, j] + CONSENSUS * NEIGHBOUR_WEIGHT * total
+            mixed_out[at] = mix[band, j] + NEIGHBOUR_WEIGHT * total
+            public_out[at] = pub[band, j]
 
 
 def solution(mesh):
@@ -196,39 +214,64 @@
         held = pltpu.VMEM((rows // TILE, col_tiles, TILE, TILE), jnp.float32)
         any_spec = pl.BlockSpec(memory_space=pl.ANY)
         smem_spec = pl.BlockSpec(memory_space=pltpu.SMEM)
-        shape = jax.ShapeDtypeStruct(banded, jnp.float32)
-        ids = block_ids.reshape(rounds, slots)
-        outs = pl.pallas_call(
+        row_tiles = rows // TILE
+        tiled = jax.ShapeDtypeStruct((row_tiles, col_tiles, TILE, TILE), jnp.float32)
+        maps_shape = (1 + SIDES, SUBLANES, TILE)
+        slots_shape = (SIDES, slots, TILE, TILE)
+        cur, pub, mix, table, arrivals = pl.pallas_call(
             functools.partial(kernel, sizes, rounds, slots),
-            out_shape=(shape, shape, shape),
-            in_specs=[smem_spec] * 4 + [any_spec] * 5,
-            out_specs=(any_spec,) * 3,
+            out_shape=(
+                tiled, tiled, tiled,
+                jax.ShapeDtypeStruct(maps_shape, jnp.int32),
+                jax.ShapeDtypeStruct(slots_shape, jnp.float32),
+            ),
+            in_specs=[any_spec] * 7,
+            out_specs=(any_spec,) * 5,
             scratch_shapes=[
+                pltpu.SMEM(block_ids.shape, jnp.int32),
+                pltpu.SMEM(block_counts.shape, jnp.int32),
                 pltpu.VMEM((tokens, rows), inputs.dtype),
                 pltpu.VMEM((tokens, cols), cotangent.dtype),
                 held, held, held,
-                pltpu.VMEM((1 + SIDES, SUBLANES, TILE), jnp.int32),
-                pltpu.SMEM((1 + SIDES, SUBLANES, TILE), jnp.int32),
-                pltpu.SemaphoreType.DMA((2 + 3 * col_tiles,)),
+                pltpu.SMEM((2, row_tiles * col_tiles), jnp.int32),
+                pltpu.VMEM(maps_shape, jnp.int32),
+                pltpu.SMEM(maps_shape, jnp.int32),
+                pltpu.SemaphoreType.DMA((4 + 3 * col_tiles,)),
                 pltpu.SemaphoreType.DMA((SIDES,)),
                 pltpu.SemaphoreType.DMA((SIDES,)),
                 pltpu.SemaphoreType.DMA,
                 pltpu.SemaphoreType.DMA((rounds, SIDES)),
                 pltpu.SemaphoreType.DMA((rounds, SIDES)),
-                pltpu.SemaphoreType.DMA((3 * col_tiles,)),
+                pltpu.SemaphoreType.DMA((4,)),
             ]
             + [pltpu.VMEM((slots + 1, TILE, TILE), jnp.float32)] * rounds
-            + [pltpu.VMEM((SIDES, slots + 1, TILE, TILE), jnp.float32)] * rounds,
+            + [pltpu.VMEM((SIDES, slots + 1, TILE, TILE), jnp.float32)] * (rounds - 1),
             compiler_params=pltpu.CompilerParams(
-                collective_id=0, has_side_effects=True, vmem_limit_bytes=48 * 1024 * 1024
+                collective_id=0, has_side_effects=True, vmem_limit_bytes=LIMIT
             ),
             cost_estimate=pl.CostEstimate(
                 flops=2 * tokens * rows * cols, bytes_accessed=6 * 4 * rows * cols, transcendentals=0
             ),
         )(
-            ids, ids // col_tiles, ids % col_tiles, block_counts.reshape(rounds),
-            params.reshape(banded), public.reshape(banded), mixed.reshape(banded), inputs, cotangent,
-        )
+            in_hbm(block_ids), in_hbm(block_counts),
+            *(in_hbm(x.reshape(banded)) for x in (params, public, mixed)),
+            in_hbm(inputs), in_hbm(cotangent),
+        )
+        group = STEP_BANDS
+        tiled_spec = pl.BlockSpec((group, col_tiles, TILE, TILE), lambda n: (n, 0, 0, 0))
+        out_spec = pl.BlockSpec((group, TILE, cols), lambda n: (n, 0, 0))
+        outs = pl.pallas_call(
+            functools.partial(finish, rounds - 1),
+            grid=(row_tiles // group,),
+            out_shape=(jax.ShapeDtypeStruct(banded, jnp.float32),) * 3,
+            in_specs=[smem_spec, tiled_spec, tiled_spec, tiled_spec]
+            + [pl.BlockSpec(slots_shape, lambda n: (0, 0, 0, 0))],
+            out_specs=(out_spec,) * 3,
+            compiler_params=pltpu.CompilerParams(vmem_limit_bytes=LIMIT),
+            cost_estimate=pl.CostEstimate(
+                flops=8 * rows * cols, bytes_accessed=8 * 4 * rows * cols, transcendentals=0
+            ),
+        )(table, cur, pub, mix, arrivals)
         return tuple(out.reshape(params.shape) for out in outs)
 
     spec = P("wide", "narrow", None, None)

time: 66.9 us -> 59.4 us (0.89)
  local copies, waits for them, and re-layouts: 8.31 us -> 0 us
  Pallas kernels: 57 us -> 58.6 us
  other arithmetic: 0.69 us -> 0 us
    unnamed x13 -> x0, local copies, waits for them, and re-layouts: 8.31 us -> none
    pallas_call x0 -> x1, Pallas kernels: none -> 4.31 us  [on_device(): pl.pallas_call(functools.partial(finish, rounds - 1), grid=(row_tiles //...]
    pallas_call x1, Pallas kernels: 57 us -> 54.3 us  [on_device(): pl.pallas_call(functools.partial(kernel, sizes, rounds, slots), out_shape...]
    select_n x1 -> x0, other arithmetic: 0.69 us -> none  [on_device(): ids % col_tiles]
where the time goes in v2:
time: 59.4 us; the launch traced here: 59.2 us
  Pallas kernels  58.6 us (99%)
  between operations  0.64 us (1%)
    pallas_call x1, Pallas kernels, on_device(): pl.pallas_call(functools.partial(kernel, sizes, rounds, slots), out_shape...  54.3 us
    pallas_call x1, Pallas kernels, on_device(): pl.pallas_call(functools.partial(finish, rounds - 1), grid=(row_tiles //...  4.31 us

profile of v2, /device:TPU:0, one launch (start us, length us, event | category | flops | bytes accessed | tf_op | source)
XLA Modules:
  0.0 59.2 jit_solution(3435030892771400043)
XLA Ops:
  0.6 54.3 %shard_map.94 = (f32[8,4,128,128]{3,2,1,0:T(8,128)S(1)}, f32[8,4,128,128]{3,2,1,0:T(8,128)S(1)}, f32[8,4,128,128]{3,2,1,0:T(8,128)S(1)}, s32[5,8,128]{2,1,0:T(8,128)S(1)}, f32[4,8,128,128]{3,2,1,0:T(8,128)S(1)}) custom-call(s32[1,1,2,8]{3,2,1,0:T(2,128)} %ids_in.1, s32[1,1,2]{2,1,0:T(1,128)} %counts_in.1, f32[8,128,512]{2,1,0:T(8,128)} %bitcast.6, ...), custom_call_target="tpu_custom_call" | custom-call | flops 268435456 | bytes 12582912 | tf_op jit(solution)/shard_map/pallas_call | solution.py:221
  54.9 4.3 %shard_map.95 = (f32[8,128,512]{2,1,0:T(8,128)}, f32[8,128,512]{2,1,0:T(8,128)}, f32[8,128,512]{2,1,0:T(8,128)}) custom-call(s32[5,8,128]{2,1,0:T(8,128)S(1)} %get-tuple-element.11.table, f32[8,4,128,128]{3,2,1,0:T(8,128)S(1)} %get-tuple-element.12.cur, f32[8,4,128,128]{3,2,1,0:T(8,128)S(1)} %get-tuple-element.13.pub, ...), custom_call_target="tpu_custom_call" | custom-call | flops 4194304 | bytes 16777216 | tf_op jit(solution)/shard_map/pallas_call | solution.py:263

commit v3 on v2

--- a/solution.py
+++ b/solution.py
@@ -11,8 +11,6 @@
 LEARN_RATE = 0.05
 NEIGHBOUR_WEIGHT = 0.2
 CONSENSUS = 0.4
-CHUNK = 256
-STEP_BANDS = 2
 LIMIT = 24 * 1024 * 1024
 SUBLANES = 8
 SIDES = 4
@@ -21,6 +19,10 @@
 
 def in_hbm(x):
     return pltpu.with_memory_space_constraint(x, pltpu.HBM)
+
+
+def in_vmem(x):
+    return pltpu.with_memory_space_constraint(x, pltpu.VMEM)
 
 
 def kernel(
@@ -31,7 +33,6 @@
 ):
     sends, recvs = buffers[:rounds], buffers[rounds:] + (last_recv,)
     row_tiles, col_tiles = cur.shape[:2]
-    rows = row_tiles * TILE
     wide, narrow = lax.axis_index("wide"), lax.axis_index("narrow")
     wide_size, narrow_size = sizes
     partners = (
@@ -45,9 +46,6 @@
         pltpu.make_async_copy(ids_in, ids, load_sem.at[2 + 3 * col_tiles]),
         pltpu.make_async_copy(counts_in, counts, load_sem.at[3 + 3 * col_tiles]),
     ]
-    load_acts = pltpu.make_async_copy(inputs.at[0, 0], acts, load_sem.at[0])
-    load_cots = pltpu.make_async_copy(cotangent.at[0, 0], cots, load_sem.at[1])
-
     def column_loads(source, held, first):
         return [
             pltpu.make_async_copy(
@@ -56,10 +54,20 @@
             for j in range(col_tiles)
         ]
 
-    load_cur = column_loads(params, cur, 2)
-    load_pub = column_loads(public, pub, 2 + col_tiles)
-    load_mix = column_loads(mixed, mix, 2 + 2 * col_tiles)
-    for load in load_lists + [load_acts, load_cots] + load_cur + load_pub + load_mix:
+    def layer_loads(source, held, first):
+        return [
+            pltpu.make_async_copy(
+                source.at[0, 0, :, pl.ds(n * TILE, TILE)], held.at[n], load_sem.at[first + n]
+            )
+            for n in range(held.shape[0])
+        ]
+
+    load_cur = column_loads(params, cur, 0)
+    load_pub = column_loads(public, pub, col_tiles)
+    load_mix = column_loads(mixed, mix, 2 * col_tiles)
+    load_layer = layer_loads(cotangent, cots, 4 + 3 * col_tiles)
+    load_layer += layer_loads(inputs, acts, 4 + 4 * col_tiles)
+    for load in load_lists + load_layer + load_cur + load_pub:
         load.start()
 
     barrier = pltpu.get_barrier_semaphore()
@@ -111,30 +119,25 @@
             total = total + recvs[r][side, map_table[1 + side, r, tile]]
         return total
 
-    load_acts.wait()
-    load_cots.wait()
-    for load in load_cur:
+    def stepped(i, j):
+        gradient = lax.dot_general(
+            acts[i], cots[j], (((0,), (0,)), ((), ())), preferred_element_type=jnp.float32
+        )
+        return cur[i, j] - LEARN_RATE * gradient
+
+    for load in load_layer + load_cur + load_pub:
         load.wait()
-    for first in range(0, rows, CHUNK):
-        gradient = lax.dot_general(
-            acts[:, first:first + CHUNK], cots[...], (((0,), (0,)), ((), ())),
-            preferred_element_type=jnp.float32,
-        )
-        for j in range(col_tiles):
-            for i in range(CHUNK // TILE):
-                part = gradient[i * TILE:(i + 1) * TILE, j * TILE:(j + 1) * TILE]
-                at = first // TILE + i
-                cur[at, j] = cur[at, j] - LEARN_RATE * part
-    for load in load_pub:
-        load.wait()
+    for load in load_mix:
+        load.start()
 
     for r in range(rounds):
         for s in range(slots):
             tile = ids[0, 0, r, s]
             i, j = places[0, tile], places[1, tile]
-            value = cur[i, j]
-            if r:
-                value = value + CONSENSUS * NEIGHBOUR_WEIGHT * arrived(r - 1, tile)
+            if r == 0:
+                value = stepped(i, j)
+            else:
+                value = cur[i, j] + CONSENSUS * NEIGHBOUR_WEIGHT * arrived(r - 1, tile)
             sends[r][s] = value - pub[i, j]
             for side in range(SIDES):
                 slot_copy(r, side, s, 1).start()
@@ -147,6 +150,13 @@
             table.wait()
             for load in load_mix:
                 load.wait()
+
+            def gradient_step(i, carry):
+                for j in range(col_tiles):
+                    cur[i, j] = stepped(i, j)
+                return carry
+
+            lax.fori_loop(0, row_tiles, gradient_step, 0)
 
         for j in range(col_tiles):
             def own_part(i, carry):
@@ -185,21 +195,53 @@
         write.wait()
 
 
-def finish(last, table, cur, pub, mix, arrivals, params_out, public_out, mixed_out):
-    bands, col_tiles = cur.shape[:2]
+def finish(
+    last, table_in, cur, pub, mix, arrivals, params_out, public_out, mixed_out,
+    table, new_cur, new_mix, table_sem, pub_sem, out_sem
+):
+    row_tiles, col_tiles = cur.shape[:2]
     slots = arrivals.shape[1]
-    for band in range(bands):
+    load = pltpu.make_async_copy(table_in, table, table_sem)
+    load.start()
+    copies = [
+        pltpu.make_async_copy(
+            pub.at[:, j], public_out.at[:, :, pl.ds(j * TILE, TILE)], pub_sem.at[j]
+        )
+        for j in range(col_tiles)
+    ]
+    for copy in copies:
+        copy.start()
+    load.wait()
+
+    def writes(i):
+        return (
+            pltpu.make_async_copy(new_cur.at[i], params_out.at[i], out_sem.at[0, i]),
+            pltpu.make_async_copy(new_mix.at[i], mixed_out.at[i], out_sem.at[1, i]),
+        )
+
+    def one_band(i, carry):
         for j in range(col_tiles):
-            tile = (pl.program_id(0) * bands + band) * col_tiles + j
             total = jnp.zeros((TILE, TILE), jnp.float32)
             for side in range(SIDES):
-                slot = table[1 + side, last, tile]
+                slot = table[1 + side, last, i * col_tiles + j]
                 part = arrivals[side, jnp.minimum(slot, slots - 1)]
                 total = total + jnp.where(slot < slots, part, 0.0)
-            at = (band, slice(None), slice(j * TILE, (j + 1) * TILE))
-            params_out[at] = cur[band, j] + CONSENSUS * NEIGHBOUR_WEIGHT * total
-            mixed_out[at] = mix[band, j] + NEIGHBOUR_WEIGHT * total
-            public_out[at] = pub[band, j]
+            span = slice(j * TILE, (j + 1) * TILE)
+            new_cur[i, :, span] = cur[i, j] + CONSENSUS * NEIGHBOUR_WEIGHT * total
+            new_mix[i, :, span] = mix[i, j] + NEIGHBOUR_WEIGHT * total
+        for write in writes(i):
+            write.start()
+        return carry
+
+    def drain(i, carry):
+        for write in writes(i):
+            write.wait()
+        return carry
+
+    lax.fori_loop(0, row_tiles, one_band, 0)
+    lax.fori_loop(0, row_tiles, drain, 0)
+    for copy in copies:
+        copy.wait()
 
 
 def solution(mesh):
@@ -213,7 +255,6 @@
         banded = (rows // TILE, TILE, cols)
         held = pltpu.VMEM((rows // TILE, col_tiles, TILE, TILE), jnp.float32)
         any_spec = pl.BlockSpec(memory_space=pl.ANY)
-        smem_spec = pl.BlockSpec(memory_space=pltpu.SMEM)
         row_tiles = rows // TILE
         tiled = jax.ShapeDtypeStruct((row_tiles, col_tiles, TILE, TILE), jnp.float32)
         maps_shape = (1 + SIDES, SUBLANES, TILE)
@@ -230,13 +271,13 @@
             scratch_shapes=[
                 pltpu.SMEM(block_ids.shape, jnp.int32),
                 pltpu.SMEM(block_counts.shape, jnp.int32),
-                pltpu.VMEM((tokens, rows), inputs.dtype),
-                pltpu.VMEM((tokens, cols), cotangent.dtype),
+                pltpu.VMEM((row_tiles, tokens, TILE), inputs.dtype),
+                pltpu.VMEM((col_tiles, tokens, TILE), cotangent.dtype),
                 held, held, held,
                 pltpu.SMEM((2, row_tiles * col_tiles), jnp.int32),
                 pltpu.VMEM(maps_shape, jnp.int32),
                 pltpu.SMEM(maps_shape, jnp.int32),
-                pltpu.SemaphoreType.DMA((4 + 3 * col_tiles,)),
+                pltpu.SemaphoreType.DMA((4 + 4 * col_tiles + row_tiles,)),
                 pltpu.SemaphoreType.DMA((SIDES,)),
                 pltpu.SemaphoreType.DMA((SIDES,)),
                 pltpu.SemaphoreType.DMA,
@@ -257,21 +298,25 @@
             *(in_hbm(x.reshape(banded)) for x in (params, public, mixed)),
             in_hbm(inputs), in_hbm(cotangent),
         )
-        group = STEP_BANDS
-        tiled_spec = pl.BlockSpec((group, col_tiles, TILE, TILE), lambda n: (n, 0, 0, 0))
-        out_spec = pl.BlockSpec((group, TILE, cols), lambda n: (n, 0, 0))
+        vmem_spec = pl.BlockSpec(memory_space=pltpu.VMEM)
         outs = pl.pallas_call(
             functools.partial(finish, rounds - 1),
-            grid=(row_tiles // group,),
             out_shape=(jax.ShapeDtypeStruct(banded, jnp.float32),) * 3,
-            in_specs=[smem_spec, tiled_spec, tiled_spec, tiled_spec]
-            + [pl.BlockSpec(slots_shape, lambda n: (0, 0, 0, 0))],
-            out_specs=(out_spec,) * 3,
+            in_specs=[any_spec, vmem_spec, any_spec, vmem_spec, vmem_spec],
+            out_specs=(any_spec,) * 3,
+            scratch_shapes=[
+                pltpu.SMEM(maps_shape, jnp.int32),
+                pltpu.VMEM(banded, jnp.float32),
+                pltpu.VMEM(banded, jnp.float32),
+                pltpu.SemaphoreType.DMA,
+                pltpu.SemaphoreType.DMA((col_tiles,)),
+                pltpu.SemaphoreType.DMA((2, row_tiles)),
+            ],
             compiler_params=pltpu.CompilerParams(vmem_limit_bytes=LIMIT),
             cost_estimate=pl.CostEstimate(
                 flops=8 * rows * cols, bytes_accessed=8 * 4 * rows * cols, transcendentals=0
             ),
-        )(table, cur, pub, mix, arrivals)
+        )(table, in_vmem(cur), pub, in_vmem(mix), in_vmem(arrivals))
         return tuple(out.reshape(params.shape) for out in outs)
 
     spec = P("wide", "narrow", None, None)

time: 59.4 us -> 58.2 us (0.980)
  Pallas kernels: 58.6 us -> 57.4 us
    pallas_call x1, Pallas kernels: 4.31 us -> 3.14 us  [on_device(): pl.pallas_call(functools.partial(finish, rounds - 1), out_shape=(jax.Shap...]
where the time goes in v3:
time: 58.2 us; the launch traced here: 58 us
  Pallas kernels  57.4 us (99%)
  between operations  0.64 us (1%)
    pallas_call x1, Pallas kernels, on_device(): pl.pallas_call(functools.partial(kernel, sizes, rounds, slots), out_shape...  54.2 us
    pallas_call x1, Pallas kernels, on_device(): pl.pallas_call(functools.partial(finish, rounds - 1), out_shape=(jax.Shap...  3.14 us

profile of v3, /device:TPU:0, one launch (start us, length us, event | category | flops | bytes accessed | tf_op | source)
XLA Modules:
  0.0 58.0 jit_solution(12634978224360473377)
XLA Ops:
  0.6 54.2 %shard_map.94 = (f32[8,4,128,128]{3,2,1,0:T(8,128)S(1)}, f32[8,4,128,128]{3,2,1,0:T(8,128)S(1)}, f32[8,4,128,128]{3,2,1,0:T(8,128)S(1)}, s32[5,8,128]{2,1,0:T(8,128)S(1)}, f32[4,8,128,128]{3,2,1,0:T(8,128)S(1)}) custom-call(s32[1,1,2,8]{3,2,1,0:T(2,128)} %ids_in.1, s32[1,1,2]{2,1,0:T(1,128)} %counts_in.1, f32[8,128,512]{2,1,0:T(8,128)} %bitcast.6, ...), custom_call_target="tpu_custom_call" | custom-call | flops 268435456 | bytes 12582912 | tf_op jit(solution)/shard_map/pallas_call | solution.py:262
  54.9 3.1 %shard_map.95 = (f32[8,128,512]{2,1,0:T(8,128)}, f32[8,128,512]{2,1,0:T(8,128)}, f32[8,128,512]{2,1,0:T(8,128)}) custom-call(s32[5,8,128]{2,1,0:T(8,128)S(1)} %get-tuple-element.11.table_in, f32[8,4,128,128]{3,2,1,0:T(8,128)S(1)} %get-tuple-element.12.cur, f32[8,4,128,128]{3,2,1,0:T(8,128)S(1)} %get-tuple-element.13.pub, ...), custom_call_target="tpu_custom_call" | custom-call | flops 4194304 | bytes 16777216 | tf_op jit(solution)/shard_map/pallas_call | solution.py:302

commit v4 on v3

--- a/solution.py
+++ b/solution.py
@@ -14,6 +14,7 @@
 LIMIT = 24 * 1024 * 1024
 SUBLANES = 8
 SIDES = 4
+NEAR = 2
 MESH = pl.DeviceIdType.MESH
 
 
@@ -31,7 +32,8 @@
     ids, counts, acts, cots, cur, pub, mix, places, maps, map_table, load_sem, map_send, map_recv, table_sem,
     send_sem, recv_sem, out_sem, *buffers
 ):
-    sends, recvs = buffers[:rounds], buffers[rounds:] + (last_recv,)
+    sends, wide_recvs = buffers[:rounds], buffers[rounds:2 * rounds]
+    narrow_recvs = buffers[2 * rounds:] + (last_recv,)
     row_tiles, col_tiles = cur.shape[:2]
     wide, narrow = lax.axis_index("wide"), lax.axis_index("narrow")
     wide_size, narrow_size = sizes
@@ -41,6 +43,10 @@
         (lax.rem(wide + 1, wide_size), narrow),
         (lax.rem(wide + wide_size - 1, wide_size), narrow),
     )
+
+    barrier = pltpu.get_barrier_semaphore()
+    for partner in partners:
+        pl.semaphore_signal(barrier, inc=1, device_id=partner, device_id_type=MESH)
 
     load_lists = [
         pltpu.make_async_copy(ids_in, ids, load_sem.at[2 + 3 * col_tiles]),
@@ -69,10 +75,6 @@
     load_layer += layer_loads(inputs, acts, 4 + 4 * col_tiles)
     for load in load_lists + load_layer + load_cur + load_pub:
         load.start()
-
-    barrier = pltpu.get_barrier_semaphore()
-    for partner in partners:
-        pl.semaphore_signal(barrier, inc=1, device_id=partner, device_id_type=MESH)
 
     row = lax.broadcasted_iota(jnp.int32, (SUBLANES, TILE), 0)
     lane = lax.broadcasted_iota(jnp.int32, (SUBLANES, TILE), 1)
@@ -86,9 +88,9 @@
     maps[0] = own_map
     for r in range(rounds):
         sends[r][slots] = jnp.zeros((TILE, TILE), jnp.float32)
-    for r in range(rounds - 1):
-        for side in range(SIDES):
-            recvs[r][side, slots] = jnp.zeros((TILE, TILE), jnp.float32)
+    for held in wide_recvs + narrow_recvs[:-1]:
+        for side in range(NEAR):
+            held[side, slots] = jnp.zeros((TILE, TILE), jnp.float32)
 
     for tile in range(row_tiles * col_tiles):
         places[0, tile] = tile // col_tiles
@@ -106,38 +108,46 @@
         copy.start()
 
     def slot_copy(r, side, first, size):
+        recvs = narrow_recvs if side < NEAR else wide_recvs
         return pltpu.make_async_remote_copy(
             src_ref=sends[r].at[pl.ds(first, size)],
-            dst_ref=recvs[r].at[side, pl.ds(first, size)],
+            dst_ref=recvs[r].at[side % NEAR, pl.ds(first, size)],
             send_sem=send_sem.at[r, side], recv_sem=recv_sem.at[r, side],
             device_id=partners[side], device_id_type=MESH,
         )
 
-    def arrived(r, tile):
-        total = recvs[r][0, map_table[1, r, tile]]
-        for side in range(1, SIDES):
-            total = total + recvs[r][side, map_table[1 + side, r, tile]]
+    def arrived(held, first_side, r, tile):
+        total = held[r][0, map_table[1 + first_side, r, tile]]
+        for side in range(1, NEAR):
+            total = total + held[r][side, map_table[1 + first_side + side, r, tile]]
         return total
 
-    def stepped(i, j):
-        gradient = lax.dot_general(
+    def gradient(i, j):
+        return lax.dot_general(
             acts[i], cots[j], (((0,), (0,)), ((), ())), preferred_element_type=jnp.float32
         )
-        return cur[i, j] - LEARN_RATE * gradient
-
-    for load in load_layer + load_cur + load_pub:
+
+    def place(r, s):
+        tile = ids[0, 0, r, s]
+        return tile, places[0, tile], places[1, tile]
+
+    for load in load_layer:
+        load.wait()
+    for s in range(slots):
+        _, i, j = place(0, s)
+        sends[0][s] = LEARN_RATE * gradient(i, j)
+    for load in load_cur + load_pub:
         load.wait()
     for load in load_mix:
         load.start()
 
     for r in range(rounds):
         for s in range(slots):
-            tile = ids[0, 0, r, s]
-            i, j = places[0, tile], places[1, tile]
+            tile, i, j = place(r, s)
             if r == 0:
-                value = stepped(i, j)
+                value = cur[i, j] - sends[r][s]
             else:
-                value = cur[i, j] + CONSENSUS * NEIGHBOUR_WEIGHT * arrived(r - 1, tile)
+                value = cur[i, j] + CONSENSUS * NEIGHBOUR_WEIGHT * arrived(narrow_recvs, 0, r - 1, tile)
             sends[r][s] = value - pub[i, j]
             for side in range(SIDES):
                 slot_copy(r, side, s, 1).start()
@@ -153,7 +163,7 @@
 
             def gradient_step(i, carry):
                 for j in range(col_tiles):
-                    cur[i, j] = stepped(i, j)
+                    cur[i, j] = cur[i, j] - LEARN_RATE * gradient(i, j)
                 return carry
 
             lax.fori_loop(0, row_tiles, gradient_step, 0)
@@ -165,7 +175,7 @@
                 new_pub = pub[i, j] + q
                 new_cur, new_mix = cur[i, j], mix[i, j]
                 if r:
-                    total = arrived(r - 1, tile)
+                    total = arrived(narrow_recvs, 0, r - 1, tile)
                     new_cur = new_cur + CONSENSUS * NEIGHBOUR_WEIGHT * total
                     q = q + total
                 new_mix = new_mix + NEIGHBOUR_WEIGHT * q
@@ -175,6 +185,18 @@
                 return carry
 
             lax.fori_loop(0, row_tiles, own_part, 0)
+
+        for side in range(NEAR, SIDES):
+            slot_copy(r, side, 0, slots).wait_recv()
+
+        def wide_part(i, carry):
+            for j in range(col_tiles):
+                total = arrived(wide_recvs, NEAR, r, i * col_tiles + j)
+                mix[i, j] = mix[i, j] + NEIGHBOUR_WEIGHT * total
+                cur[i, j] = cur[i, j] + CONSENSUS * NEIGHBOUR_WEIGHT * total
+            return carry
+
+        lax.fori_loop(0, row_tiles, wide_part, 0)
 
         if r == rounds - 1:
             writes = [
@@ -185,7 +207,7 @@
             ]
             for write in writes:
                 write.start()
-        for side in range(SIDES):
+        for side in range(NEAR):
             slot_copy(r, side, 0, slots).wait_recv()
 
     for r in range(rounds):
@@ -222,7 +244,7 @@
     def one_band(i, carry):
         for j in range(col_tiles):
             total = jnp.zeros((TILE, TILE), jnp.float32)
-            for side in range(SIDES):
+            for side in range(NEAR):
                 slot = table[1 + side, last, i * col_tiles + j]
                 part = arrivals[side, jnp.minimum(slot, slots - 1)]
                 total = total + jnp.where(slot < slots, part, 0.0)
@@ -258,7 +280,7 @@
         row_tiles = rows // TILE
         tiled = jax.ShapeDtypeStruct((row_tiles, col_tiles, TILE, TILE), jnp.float32)
         maps_shape = (1 + SIDES, SUBLANES, TILE)
-        slots_shape = (SIDES, slots, TILE, TILE)
+        slots_shape = (NEAR, slots, TILE, TILE)
         cur, pub, mix, table, arrivals = pl.pallas_call(
             functools.partial(kernel, sizes, rounds, slots),
             out_shape=(
@@ -286,7 +308,7 @@
                 pltpu.SemaphoreType.DMA((4,)),
             ]
             + [pltpu.VMEM((slots + 1, TILE, TILE), jnp.float32)] * rounds
-            + [pltpu.VMEM((SIDES, slots + 1, TILE, TILE), jnp.float32)] * (rounds - 1),
+            + [pltpu.VMEM((NEAR, slots + 1, TILE, TILE), jnp.float32)] * (2 * rounds - 1),
             compiler_params=pltpu.CompilerParams(
                 collective_id=0, has_side_effects=True, vmem_limit_bytes=LIMIT
             ),

time: 58.2 us -> 58.2 us (level)
  no operation moved by 1% of the time
where the time goes in v4:
time: 58.2 us; the launch traced here: 58 us
  Pallas kernels  57.4 us (99%)
  between operations  0.64 us (1%)
    pallas_call x1, Pallas kernels, on_device(): pl.pallas_call(functools.partial(kernel, sizes, rounds, slots), out_shape...  54.3 us
    pallas_call x1, Pallas kernels, on_device(): pl.pallas_call(functools.partial(finish, rounds - 1), out_shape=(jax.Shap...  3.09 us

profile of v4, /device:TPU:0, one launch (start us, length us, event | category | flops | bytes accessed | tf_op | source)
XLA Modules:
  0.0 58.0 jit_solution(6368163717040857354)
XLA Ops:
  0.6 54.3 %shard_map.94 = (f32[8,4,128,128]{3,2,1,0:T(8,128)S(1)}, f32[8,4,128,128]{3,2,1,0:T(8,128)S(1)}, f32[8,4,128,128]{3,2,1,0:T(8,128)S(1)}, s32[5,8,128]{2,1,0:T(8,128)S(1)}, f32[2,8,128,128]{3,2,1,0:T(8,128)S(1)}) custom-call(s32[1,1,2,8]{3,2,1,0:T(2,128)} %ids_in.1, s32[1,1,2]{2,1,0:T(1,128)} %counts_in.1, f32[8,128,512]{2,1,0:T(8,128)} %bitcast.6, ...), custom_call_target="tpu_custom_call" | custom-call | flops 268435456 | bytes 12582912 | tf_op jit(solution)/shard_map/pallas_call | solution.py:284
  55.0 3.1 %shard_map.95 = (f32[8,128,512]{2,1,0:T(8,128)}, f32[8,128,512]{2,1,0:T(8,128)}, f32[8,128,512]{2,1,0:T(8,128)}) custom-call(s32[5,8,128]{2,1,0:T(8,128)S(1)} %get-tuple-element.11.table_in, f32[8,4,128,128]{3,2,1,0:T(8,128)S(1)} %get-tuple-element.12.cur, f32[8,4,128,128]{3,2,1,0:T(8,128)S(1)} %get-tuple-element.13.pub, ...), custom_call_target="tpu_custom_call" | custom-call | flops 4194304 | bytes 16777216 | tf_op jit(solution)/shard_map/pallas_call | solution.py:324

commit v5 on v4

--- a/solution.py
+++ b/solution.py
@@ -149,8 +149,10 @@
             else:
                 value = cur[i, j] + CONSENSUS * NEIGHBOUR_WEIGHT * arrived(narrow_recvs, 0, r - 1, tile)
             sends[r][s] = value - pub[i, j]
-            for side in range(SIDES):
+            for side in range(NEAR):
                 slot_copy(r, side, s, 1).start()
+        for side in range(NEAR, SIDES):
+            slot_copy(r, side, 0, slots).start()
 
         if r == 0:
             for copy in map_copies:

time: 58.2 us -> 58.2 us (level)
  no operation moved by 1% of the time
where the time goes in v5:
time: 58.2 us; the launch traced here: 58 us
  Pallas kernels  57.4 us (99%)
  between operations  0.64 us (1%)
    pallas_call x1, Pallas kernels, on_device(): pl.pallas_call(functools.partial(kernel, sizes, rounds, slots), out_shape...  54.3 us
    pallas_call x1, Pallas kernels, on_device(): pl.pallas_call(functools.partial(finish, rounds - 1), out_shape=(jax.Shap...  3.09 us

profile of v5, /device:TPU:0, one launch (start us, length us, event | category | flops | bytes accessed | tf_op | source)
XLA Modules:
  0.0 58.0 jit_solution(15442341892563840443)
XLA Ops:
  0.6 54.3 %shard_map.94 = (f32[8,4,128,128]{3,2,1,0:T(8,128)S(1)}, f32[8,4,128,128]{3,2,1,0:T(8,128)S(1)}, f32[8,4,128,128]{3,2,1,0:T(8,128)S(1)}, s32[5,8,128]{2,1,0:T(8,128)S(1)}, f32[2,8,128,128]{3,2,1,0:T(8,128)S(1)}) custom-call(s32[1,1,2,8]{3,2,1,0:T(2,128)} %ids_in.1, s32[1,1,2]{2,1,0:T(1,128)} %counts_in.1, f32[8,128,512]{2,1,0:T(8,128)} %bitcast.6, ...), custom_call_target="tpu_custom_call" | custom-call | flops 268435456 | bytes 12582912 | tf_op jit(solution)/shard_map/pallas_call | solution.py:286
  55.0 3.1 %shard_map.95 = (f32[8,128,512]{2,1,0:T(8,128)}, f32[8,128,512]{2,1,0:T(8,128)}, f32[8,128,512]{2,1,0:T(8,128)}) custom-call(s32[5,8,128]{2,1,0:T(8,128)S(1)} %get-tuple-element.11.table_in, f32[8,4,128,128]{3,2,1,0:T(8,128)S(1)} %get-tuple-element.12.cur, f32[8,4,128,128]{3,2,1,0:T(8,128)S(1)} %get-tuple-element.13.pub, ...), custom_call_target="tpu_custom_call" | custom-call | flops 4194304 | bytes 16777216 | tf_op jit(solution)/shard_map/pallas_call | solution.py:326

commit v6 on v4

--- a/solution.py
+++ b/solution.py
@@ -96,7 +96,6 @@
         places[0, tile] = tile // col_tiles
         places[1, tile] = tile % col_tiles
 
-    pl.semaphore_wait(barrier, SIDES)
     map_copies = [
         pltpu.make_async_remote_copy(
             src_ref=maps.at[0], dst_ref=maps.at[1 + side], send_sem=map_send.at[side],
@@ -104,8 +103,6 @@
         )
         for side in range(SIDES)
     ]
-    for copy in map_copies:
-        copy.start()
 
     def slot_copy(r, side, first, size):
         recvs = narrow_recvs if side < NEAR else wide_recvs
@@ -149,6 +146,10 @@
             else:
                 value = cur[i, j] + CONSENSUS * NEIGHBOUR_WEIGHT * arrived(narrow_recvs, 0, r - 1, tile)
             sends[r][s] = value - pub[i, j]
+            if r == 0 and s == 0:
+                pl.semaphore_wait(barrier, SIDES)
+                for copy in map_copies:
+                    copy.start()
             for side in range(SIDES):
                 slot_copy(r, side, s, 1).start()
 

time: 58.2 us -> 57.8 us (level)
  no operation moved by 1% of the time
where the time goes in v6:
time: 57.8 us; the launch traced here: 57.6 us
  Pallas kernels  57 us (99%)
  between operations  0.64 us (1%)
    pallas_call x1, Pallas kernels, on_device(): pl.pallas_call(functools.partial(kernel, sizes, rounds, slots), out_shape...  53.9 us
    pallas_call x1, Pallas kernels, on_device(): pl.pallas_call(functools.partial(finish, rounds - 1), out_shape=(jax.Shap...  3.09 us

profile of v6, /device:TPU:0, one launch (start us, length us, event | category | flops | bytes accessed | tf_op | source)
XLA Modules:
  0.0 57.6 jit_solution(358601306385255574)
XLA Ops:
  0.6 53.9 %shard_map.94 = (f32[8,4,128,128]{3,2,1,0:T(8,128)S(1)}, f32[8,4,128,128]{3,2,1,0:T(8,128)S(1)}, f32[8,4,128,128]{3,2,1,0:T(8,128)S(1)}, s32[5,8,128]{2,1,0:T(8,128)S(1)}, f32[2,8,128,128]{3,2,1,0:T(8,128)S(1)}) custom-call(s32[1,1,2,8]{3,2,1,0:T(2,128)} %ids_in.1, s32[1,1,2]{2,1,0:T(1,128)} %counts_in.1, f32[8,128,512]{2,1,0:T(8,128)} %bitcast.6, ...), custom_call_target="tpu_custom_call" | custom-call | flops 268435456 | bytes 12582912 | tf_op jit(solution)/shard_map/pallas_call | solution.py:285
  54.5 3.1 %shard_map.95 = (f32[8,128,512]{2,1,0:T(8,128)}, f32[8,128,512]{2,1,0:T(8,128)}, f32[8,128,512]{2,1,0:T(8,128)}) custom-call(s32[5,8,128]{2,1,0:T(8,128)S(1)} %get-tuple-element.11.table_in, f32[8,4,128,128]{3,2,1,0:T(8,128)S(1)} %get-tuple-element.12.cur, f32[8,4,128,128]{3,2,1,0:T(8,128)S(1)} %get-tuple-element.13.pub, ...), custom_call_target="tpu_custom_call" | custom-call | flops 4194304 | bytes 16777216 | tf_op jit(solution)/shard_map/pallas_call | solution.py:325

commit v7 on v6

--- a/solution.py
+++ b/solution.py
@@ -203,8 +203,14 @@
             writes = [
                 pltpu.make_async_copy(held, target, out_sem.at[n])
                 for n, (held, target) in enumerate(
-                    ((cur, cur_out), (pub, pub_out), (mix, mix_out), (maps, maps_out))
+                    ((cur, cur_out), (mix, mix_out), (maps, maps_out))
                 )
+            ]
+            writes += [
+                pltpu.make_async_copy(
+                    pub.at[:, j], pub_out.at[:, :, pl.ds(j * TILE, TILE)], out_sem.at[3 + j]
+                )
+                for j in range(col_tiles)
             ]
             for write in writes:
                 write.start()
@@ -227,10 +233,8 @@
     load = pltpu.make_async_copy(table_in, table, table_sem)
     load.start()
     copies = [
-        pltpu.make_async_copy(
-            pub.at[:, j], public_out.at[:, :, pl.ds(j * TILE, TILE)], pub_sem.at[j]
-        )
-        for j in range(col_tiles)
+        pltpu.make_async_copy(pub.at[i], public_out.at[i], pub_sem.at[i])
+        for i in range(row_tiles)
     ]
     for copy in copies:
         copy.start()
@@ -285,7 +289,7 @@
         cur, pub, mix, table, arrivals = pl.pallas_call(
             functools.partial(kernel, sizes, rounds, slots),
             out_shape=(
-                tiled, tiled, tiled,
+                tiled, jax.ShapeDtypeStruct(banded, jnp.float32), tiled,
                 jax.ShapeDtypeStruct(maps_shape, jnp.int32),
                 jax.ShapeDtypeStruct(slots_shape, jnp.float32),
             ),
@@ -306,7 +310,7 @@
                 pltpu.SemaphoreType.DMA,
                 pltpu.SemaphoreType.DMA((rounds, SIDES)),
                 pltpu.SemaphoreType.DMA((rounds, SIDES)),
-                pltpu.SemaphoreType.DMA((4,)),
+                pltpu.SemaphoreType.DMA((3 + col_tiles,)),
             ]
             + [pltpu.VMEM((slots + 1, TILE, TILE), jnp.float32)] * rounds
             + [pltpu.VMEM((NEAR, slots + 1, TILE, TILE), jnp.float32)] * (2 * rounds - 1),
@@ -332,7 +336,7 @@
                 pltpu.VMEM(banded, jnp.float32),
                 pltpu.VMEM(banded, jnp.float32),
                 pltpu.SemaphoreType.DMA,
-                pltpu.SemaphoreType.DMA((col_tiles,)),
+                pltpu.SemaphoreType.DMA((row_tiles,)),
                 pltpu.SemaphoreType.DMA((2, row_tiles)),
             ],
             compiler_params=pltpu.CompilerParams(vmem_limit_bytes=LIMIT),

time: 57.8 us -> 57.9 us (level)
  no operation moved by 1% of the time
where the time goes in v7:
time: 57.9 us; the launch traced here: 57.7 us
  Pallas kernels  57.1 us (99%)
  between operations  0.64 us (1%)
    pallas_call x1, Pallas kernels, on_device(): pl.pallas_call(functools.partial(kernel, sizes, rounds, slots), out_shape...  53.9 us
    pallas_call x1, Pallas kernels, on_device(): pl.pallas_call(functools.partial(finish, rounds - 1), out_shape=(jax.Shap...  3.14 us

profile of v7, /device:TPU:0, one launch (start us, length us, event | category | flops | bytes accessed | tf_op | source)
XLA Modules:
  0.0 57.7 jit_solution(4182025079508324678)
XLA Ops:
  0.6 53.9 %shard_map.94 = (f32[8,4,128,128]{3,2,1,0:T(8,128)S(1)}, f32[8,128,512]{2,1,0:T(8,128)S(1)}, f32[8,4,128,128]{3,2,1,0:T(8,128)S(1)}, s32[5,8,128]{2,1,0:T(8,128)S(1)}, f32[2,8,128,128]{3,2,1,0:T(8,128)S(1)}) custom-call(s32[1,1,2,8]{3,2,1,0:T(2,128)} %ids_in.1, s32[1,1,2]{2,1,0:T(1,128)} %counts_in.1, f32[8,128,512]{2,1,0:T(8,128)} %bitcast.6, ...), custom_call_target="tpu_custom_call" | custom-call | flops 268435456 | bytes 12582912 | tf_op jit(solution)/shard_map/pallas_call | solution.py:289
  54.6 3.1 %shard_map.95 = (f32[8,128,512]{2,1,0:T(8,128)}, f32[8,128,512]{2,1,0:T(8,128)}, f32[8,128,512]{2,1,0:T(8,128)}) custom-call(s32[5,8,128]{2,1,0:T(8,128)S(1)} %get-tuple-element.11.table_in, f32[8,4,128,128]{3,2,1,0:T(8,128)S(1)} %get-tuple-element.12.cur, f32[8,128,512]{2,1,0:T(8,128)S(1)} %get-tuple-element.13.pub, ...), custom_call_target="tpu_custom_call" | custom-call | flops 4194304 | bytes 16777216 | tf_op jit(solution)/shard_map/pallas_call | solution.py:329

commit v8 on v7

--- a/solution.py
+++ b/solution.py
@@ -130,7 +130,8 @@
 
     for load in load_layer:
         load.wait()
-    for s in range(slots):
+    early = (slots + 1) // 2
+    for s in range(early):
         _, i, j = place(0, s)
         sends[0][s] = LEARN_RATE * gradient(i, j)
     for load in load_cur + load_pub:
@@ -142,7 +143,7 @@
         for s in range(slots):
             tile, i, j = place(r, s)
             if r == 0:
-                value = cur[i, j] - sends[r][s]
+                value = cur[i, j] - (sends[r][s] if s < early else LEARN_RATE * gradient(i, j))
             else:
                 value = cur[i, j] + CONSENSUS * NEIGHBOUR_WEIGHT * arrived(narrow_recvs, 0, r - 1, tile)
             sends[r][s] = value - pub[i, j]

time: 57.9 us -> 57.9 us (level)
  no operation moved by 1% of the time
where the time goes in v8:
time: 57.9 us; the launch traced here: 57.7 us
  Pallas kernels  57.1 us (99%)
  between operations  0.64 us (1%)
    pallas_call x1, Pallas kernels, on_device(): pl.pallas_call(functools.partial(kernel, sizes, rounds, slots), out_shape...  53.9 us
    pallas_call x1, Pallas kernels, on_device(): pl.pallas_call(functools.partial(finish, rounds - 1), out_shape=(jax.Shap...  3.15 us

profile of v8, /device:TPU:0, one launch (start us, length us, event | category | flops | bytes accessed | tf_op | source)
XLA Modules:
  0.0 57.7 jit_solution(15741050126714146939)
XLA Ops:
  0.6 53.9 %shard_map.94 = (f32[8,4,128,128]{3,2,1,0:T(8,128)S(1)}, f32[8,128,512]{2,1,0:T(8,128)S(1)}, f32[8,4,128,128]{3,2,1,0:T(8,128)S(1)}, s32[5,8,128]{2,1,0:T(8,128)S(1)}, f32[2,8,128,128]{3,2,1,0:T(8,128)S(1)}) custom-call(s32[1,1,2,8]{3,2,1,0:T(2,128)} %ids_in.1, s32[1,1,2]{2,1,0:T(1,128)} %counts_in.1, f32[8,128,512]{2,1,0:T(8,128)} %bitcast.6, ...), custom_call_target="tpu_custom_call" | custom-call | flops 268435456 | bytes 12582912 | tf_op jit(solution)/shard_map/pallas_call | solution.py:290
  54.6 3.1 %shard_map.95 = (f32[8,128,512]{2,1,0:T(8,128)}, f32[8,128,512]{2,1,0:T(8,128)}, f32[8,128,512]{2,1,0:T(8,128)}) custom-call(s32[5,8,128]{2,1,0:T(8,128)S(1)} %get-tuple-element.11.table_in, f32[8,4,128,128]{3,2,1,0:T(8,128)S(1)} %get-tuple-element.12.cur, f32[8,128,512]{2,1,0:T(8,128)S(1)} %get-tuple-element.13.pub, ...), custom_call_target="tpu_custom_call" | custom-call | flops 4194304 | bytes 16777216 | tf_op jit(solution)/shard_map/pallas_call | solution.py:330
